TPU v7x, 32 devices: a whole 2x2x4 slice. The times are simulated.
32 devices in a mesh: dp: 4 (over y, x), seq: 8 (over z, core).
Axes of the slice: x: 2, y: 2, z: 4, core: 2. Of those that a mesh axis runs over, the one named last changes fastest.
Arguments:
- char_ids: int32 [4, 4096], P('dp', 'seq'), may hold values from 0 to 255
- seg_starts: int32 [4, 8], P('dp', 'seq'), may hold values from 0 to 1, as said below
- char_table: bfloat16 [256, 1024], replicated, may hold values from -6 to 6
- norm_gain: float32 [1024], replicated, may hold values from 0.5 to 1.5
- qkv_weight: bfloat16 [1024, 3072], replicated, may hold values from -0.1875 to 0.1875
- distance_bias: float32 [256], replicated, may hold values from -3 to 3
- state_query: bfloat16 [512, 1024], replicated, may hold values from -9 to 9
- state_init: bfloat16 [512, 1024], replicated, may hold values from -6 to 6
- state_gain: float32 [1024], replicated, may hold values from 0.5 to 1.5
- state_kv_weight: bfloat16 [1024, 2048], replicated, may hold values from -0.1875 to 0.1875
- gate_logit: float32 [1024], replicated, may hold values from 0 to 6
- out_weight: bfloat16 [1024, 1024], replicated, may hold values from -1.5 to 1.5
- mlp_gain: float32 [1024], replicated, may hold values from 0.5 to 1.5
- up_weight: bfloat16 [1024, 4096], replicated, may hold values from -0.1875 to 0.1875
- down_weight: bfloat16 [4096, 1024], replicated, may hold values from -0.1875 to 0.1875
- cotangent: bfloat16 [4, 4096, 1024], P('dp', 'seq'), may hold values from -6 to 6
Outputs:
- layer_out: bfloat16 [4, 4096, 1024], P('dp', 'seq')
- grad_table: float32 [256, 1024], P('seq')
- grad_norm_gain: float32 [1024], P('seq')
- grad_qkv: float32 [1024, 3072], P('seq')
- grad_distance_bias: float32 [256], P('seq')
- grad_state_query: float32 [512, 1024], P('seq')
- grad_state_init: float32 [512, 1024], P('seq')
- grad_state_gain: float32 [1024], P('seq')
- grad_state_kv: float32 [1024, 2048], P('seq')
- grad_gate: float32 [1024], P('seq')
- grad_out: float32 [1024, 1024], P('seq')
- grad_mlp_gain: float32 [1024], P('seq')
- grad_up: float32 [1024, 4096], P('seq')
- grad_down: float32 [4096, 1024], P('seq')
Inputs may be any that keep to these rules, and one draw needn't show every extreme that they name: `seg_starts`: the first window of every row is marked; one of the 4 rows has no other mark.
All inputs are finite; a program needn't handle non-finite values.
Results may differ from a plain program's by a relative error of at most 0.034.
Values may be sent and summed in bfloat16 or wider, within the bound.
No kernel may reach another device: no remote copies, remote signals or barrier semaphores. Data moves between devices by JAX's collectives and lax.ppermute only.
A program may use at most 448 MiB of HBM per device.

v0:
```python
import math

import jax
import jax.numpy as jnp
import numpy as np
from jax import lax
from jax.sharding import PartitionSpec as P

D = 1024
HEADS = 8
HEAD_DIM = 128
VOCAB = 256
STATES = 512
WINDOW = 512
BUCKETS = 32
MAX_DISTANCE = 128


epsilon = 1e-05
highest = lax.Precision.HIGHEST
hidden_mask = -1e30


def from_behind(block, axis, distance):
    devices = range(lax.axis_size(axis))
    route = [(i - distance, i) for i in devices if i - distance in devices]
    return lax.ppermute(block, axis, route)


def entering(value, axis, combine, identity):
    length, here = (lax.axis_size(axis), lax.axis_index(axis))
    everything = jax.tree.map(lambda part: lax.all_gather(part, axis), value)
    start = jax.tree.map(
        lambda part, zero: jnp.broadcast_to(jnp.asarray(zero, part.dtype), part.shape),
        value,
        identity,
    )

    def lap(k, before):
        reached = k < here
        new = combine(before, jax.tree.map(lambda part: part[k], everything))
        return jax.tree.map(lambda a, b: jnp.where(reached, a, b), new, before)

    return lax.fori_loop(0, length, lap, start)


def entering_2(value, axis, combine, identity):
    length, here = (lax.axis_size(axis), lax.axis_index(axis))
    everything = jax.tree.map(
        lambda part, kind: lax.all_gather(part.astype(kind), axis),
        value,
        jax.tree.map(lambda a: jnp.bfloat16 if a.dtype == jnp.float32 else a.dtype, value),
    )
    start = jax.tree.map(
        lambda part, zero: jnp.broadcast_to(jnp.asarray(zero, part.dtype), part.shape),
        value,
        identity,
    )

    def lap(k, before):
        at = length - 1 - k
        reached = at > here
        new = combine(
            before, jax.tree.map(lambda part, own: part[at].astype(own.dtype), everything, value)
        )
        return jax.tree.map(lambda a, b: jnp.where(reached, a, b), new, before)

    return lax.fori_loop(0, length, lap, start)


def layer_norm(value, gain):
    centre = jnp.mean(value, axis=-1, keepdims=True)
    offset = value - centre
    spread = jnp.mean(offset * offset, axis=-1, keepdims=True)
    return offset * lax.rsqrt(spread + epsilon) * gain


def norm_back(value, gain, upstream):
    _, pullback = jax.vjp(layer_norm, value, gain)
    return pullback(upstream)


def bucket_table():
    distance = np.arange(WINDOW)
    exact_count = BUCKETS // 2
    log_ratio = np.log(np.maximum(distance, 1) / exact_count) / math.log(MAX_DISTANCE / exact_count)
    far_bucket = exact_count + np.floor(log_ratio * (BUCKETS - exact_count)).astype(np.int64)
    return np.where(distance < exact_count, distance, np.minimum(far_bucket, BUCKETS - 1))


def bucket_pick():
    return (bucket_table()[None, :] == np.arange(BUCKETS)[:, None]).astype(np.float32)


def visible_mask():
    query_pos = np.arange(WINDOW)[:, None]
    key_pos = np.arange(2 * WINDOW)[None, :]
    distance = WINDOW + query_pos - key_pos
    return (distance >= 0) & (distance < WINDOW)


def bias_matrix(distance_bias):
    table = jnp.dot(
        distance_bias.reshape(HEADS, BUCKETS),
        jnp.asarray(bucket_pick()),
        precision=highest,
        preferred_element_type=jnp.float32,
    )
    blank = jnp.zeros((HEADS, WINDOW), jnp.float32)
    padded = jnp.concatenate([blank, table[:, ::-1], blank], axis=1)
    tiled = jnp.tile(padded, (1, WINDOW))[:, : WINDOW * (3 * WINDOW - 1)]
    return tiled.reshape(HEADS, WINDOW, 3 * WINDOW - 1)[:, :, WINDOW - 1 :]


def bias_fold(grad_matrix):
    blank = jnp.zeros((HEADS, WINDOW, WINDOW - 1), jnp.float32)
    flat = jnp.concatenate([blank, grad_matrix], axis=2).reshape(HEADS, -1)
    flat = jnp.concatenate([flat, jnp.zeros((HEADS, WINDOW), jnp.float32)], axis=1)
    folded = jnp.sum(flat.reshape(HEADS, WINDOW, 3 * WINDOW), axis=1)
    by_distance = folded[:, WINDOW : 2 * WINDOW][:, ::-1]
    picked = lax.dot_general(
        by_distance,
        jnp.asarray(bucket_pick()),
        (((1,), (1,)), ((), ())),
        precision=highest,
        preferred_element_type=jnp.float32,
    )
    return picked.reshape(-1)


def masked_scores(query_lane, keys_lane, live_lane, full_bias, token_mask):
    score_scale = 1.0 / math.sqrt(HEAD_DIM)
    scores = (
        jnp.einsum("qhd,khd->hqk", query_lane, keys_lane, preferred_element_type=jnp.float32)
        * score_scale
        + full_bias
    )
    halo_ok = jnp.logical_and(jnp.asarray(token_mask[:, :WINDOW]), live_lane > 0.5)
    visible = jnp.concatenate(
        [halo_ok, jnp.asarray(token_mask[:, WINDOW:]), jnp.ones((WINDOW, STATES), jnp.bool_)],
        axis=1,
    )
    return jnp.where(visible[None], scores, hidden_mask)


def compose(earlier, later):
    return (earlier[0] * later[0], later[0][:, None, :] * earlier[1] + later[1])


def body(
    char_ids,
    seg_starts,
    char_table,
    norm_gain,
    qkv_weight,
    distance_bias,
    state_query,
    state_init,
    state_gain,
    state_kv_weight,
    gate_logit,
    out_weight,
    mlp_gain,
    up_weight,
    down_weight,
    cotangent,
):
    lane_count = char_ids.shape[0]
    token_rows = lane_count * WINDOW
    score_scale = 1.0 / math.sqrt(HEAD_DIM)
    onehot = (char_ids.reshape(-1, 1) == jnp.arange(VOCAB, dtype=jnp.int32)[None, :]).astype(
        jnp.bfloat16
    )
    tokens = jnp.dot(onehot, char_table, preferred_element_type=jnp.float32)
    normed = layer_norm(tokens, norm_gain).astype(jnp.bfloat16)
    qkv = jnp.dot(normed, qkv_weight, preferred_element_type=jnp.float32).astype(jnp.bfloat16)
    qkv = qkv.reshape(lane_count, WINDOW, 3, HEADS, HEAD_DIM)
    queries = qkv[:, :, 0]
    own_kv = qkv[:, :, 1:]
    prev_kv = from_behind(own_kv, "seq", 1)
    start_flag = seg_starts[:, 0].astype(jnp.float32)
    halo_live = 1.0 - start_flag
    query_state = state_query.reshape(STATES, HEADS, HEAD_DIM)
    own_keys = own_kv[:, :, 0]
    own_values = own_kv[:, :, 1]
    summary_scores = (
        jnp.einsum("shd,lthd->lhst", query_state, own_keys, preferred_element_type=jnp.float32)
        * score_scale
    )
    summary_peak = jnp.max(summary_scores, axis=-1, keepdims=True)
    summary_exp = jnp.exp(summary_scores - summary_peak)
    summary_probs = summary_exp / jnp.sum(summary_exp, axis=-1, keepdims=True)
    summary_weights = summary_probs.astype(jnp.bfloat16)
    updates = jnp.einsum(
        "lhst,lthd->lshd", summary_weights, own_values, preferred_element_type=jnp.float32
    ).reshape(lane_count, STATES, D)
    forget = jax.nn.sigmoid(gate_logit)
    init_state = state_init.astype(jnp.float32)
    carry_scale = halo_live[:, None] * forget[None, :]
    carry_shift = start_flag[:, None, None] * (forget * init_state)[None] + (1.0 - forget) * updates
    identity = (jnp.ones_like(carry_scale), jnp.zeros_like(carry_shift))
    prefix = entering((carry_scale, carry_shift), "seq", compose, identity)
    states_in = jnp.where(start_flag[:, None, None] > 0.5, init_state[None], prefix[1])
    state_normed = layer_norm(states_in, state_gain).astype(jnp.bfloat16).reshape(-1, D)
    state_kv = jnp.dot(state_normed, state_kv_weight, preferred_element_type=jnp.float32).astype(
        jnp.bfloat16
    )
    state_kv = state_kv.reshape(lane_count, STATES, 2, HEADS, HEAD_DIM)
    context = jnp.concatenate([prev_kv, own_kv, state_kv], axis=1)
    full_bias = jnp.concatenate(
        [bias_matrix(distance_bias), jnp.zeros((HEADS, WINDOW, STATES), jnp.float32)], axis=2
    )
    token_mask = visible_mask()

    def attend(items):
        query_lane, context_lane, live_lane = items
        scores = masked_scores(query_lane, context_lane[:, 0], live_lane, full_bias, token_mask)
        row_peak = jnp.max(scores, axis=-1, keepdims=True)
        raised = jnp.exp(scores - row_peak)
        row_total = jnp.sum(raised, axis=-1, keepdims=True)
        attention = (raised / row_total).astype(jnp.bfloat16)
        mixed = jnp.einsum(
            "hqk,khd->qhd", attention, context_lane[:, 1], preferred_element_type=jnp.float32
        )
        return (mixed.astype(jnp.bfloat16), row_peak + jnp.log(row_total))

    mixed_heads, vertical_lse = lax.map(attend, (queries, context, halo_live))
    mixed_rows = mixed_heads.reshape(token_rows, D)
    attention_out = jnp.dot(mixed_rows, out_weight, preferred_element_type=jnp.float32)
    residual = tokens + attention_out
    mlp_in = layer_norm(residual, mlp_gain).astype(jnp.bfloat16)
    pre_act = jnp.dot(mlp_in, up_weight, preferred_element_type=jnp.float32)
    act_low = jax.nn.gelu(pre_act).astype(jnp.bfloat16)
    layer_out = (
        residual + jnp.dot(act_low, down_weight, preferred_element_type=jnp.float32)
    ).astype(jnp.bfloat16)
    layer_out = layer_out.reshape(lane_count, WINDOW, D)
    upstream = cotangent.reshape(token_rows, D)
    grad_down = jnp.dot(act_low.T, upstream, preferred_element_type=jnp.float32)
    grad_act = jnp.dot(upstream, down_weight.T, preferred_element_type=jnp.float32)
    _, gelu_back = jax.vjp(jax.nn.gelu, pre_act)
    grad_pre = gelu_back(grad_act)[0].astype(jnp.bfloat16)
    grad_up = jnp.dot(mlp_in.T, grad_pre, preferred_element_type=jnp.float32)
    grad_mlp_in = jnp.dot(grad_pre, up_weight.T, preferred_element_type=jnp.float32)
    grad_res_norm, grad_mlp_gain = norm_back(residual, mlp_gain, grad_mlp_in)
    grad_residual = upstream.astype(jnp.float32) + grad_res_norm
    grad_attention = grad_residual.astype(jnp.bfloat16)
    grad_out = jnp.dot(mixed_rows.T, grad_attention, preferred_element_type=jnp.float32)
    grad_mixed = jnp.dot(grad_attention, out_weight.T, preferred_element_type=jnp.float32).astype(
        jnp.bfloat16
    )
    grad_mixed = grad_mixed.reshape(lane_count, WINDOW, HEADS, HEAD_DIM)

    def attend_back(items):
        query_lane, context_lane, live_lane, lse_lane, grad_lane = items
        keys_lane = context_lane[:, 0]
        values_lane = context_lane[:, 1]
        scores = masked_scores(query_lane, keys_lane, live_lane, full_bias, token_mask)
        attention = jnp.exp(scores - lse_lane)
        attention_low = attention.astype(jnp.bfloat16)
        grad_values = jnp.einsum(
            "hqk,qhd->khd", attention_low, grad_lane, preferred_element_type=jnp.float32
        )
        grad_weights = jnp.einsum(
            "qhd,khd->hqk", grad_lane, values_lane, preferred_element_type=jnp.float32
        )
        row_inner = jnp.sum(attention * grad_weights, axis=-1, keepdims=True)
        grad_scores = (attention * (grad_weights - row_inner)).astype(jnp.bfloat16)
        grad_query = (
            jnp.einsum("hqk,khd->qhd", grad_scores, keys_lane, preferred_element_type=jnp.float32)
            * score_scale
        )
        grad_keys = (
            jnp.einsum("hqk,qhd->khd", grad_scores, query_lane, preferred_element_type=jnp.float32)
            * score_scale
        )
        return (
            grad_query,
            jnp.stack([grad_keys, grad_values], axis=1),
            grad_scores[:, :, : 2 * WINDOW],
        )

    grad_queries, grad_context, grad_bias_lanes = lax.map(
        attend_back, (queries, context, halo_live, vertical_lse, grad_mixed)
    )
    from_next = from_behind(grad_context[:, :WINDOW].astype(jnp.bfloat16), "seq", -1).astype(
        jnp.float32
    )
    grad_own = grad_context[:, WINDOW : 2 * WINDOW] + from_next
    grad_state_rows = (
        grad_context[:, 2 * WINDOW :].reshape(lane_count * STATES, 2 * D).astype(jnp.bfloat16)
    )
    grad_state_kv = jnp.dot(state_normed.T, grad_state_rows, preferred_element_type=jnp.float32)
    grad_state_normed = jnp.dot(
        grad_state_rows, state_kv_weight.T, preferred_element_type=jnp.float32
    ).reshape(lane_count, STATES, D)
    local_grad, grad_state_gain = norm_back(states_in, state_gain, grad_state_normed)
    back_shift = halo_live[:, None, None] * local_grad
    suffix = entering_2((carry_scale, back_shift), "seq", compose, identity)
    after = suffix[1]
    total_in = local_grad + forget * after
    grad_state_init = jnp.sum(start_flag[:, None, None] * total_in, axis=0)
    grad_gate = jnp.sum(after * (states_in - updates), axis=(0, 1)) * forget * (1.0 - forget)
    grad_update = (
        ((1.0 - forget) * after).astype(jnp.bfloat16).reshape(lane_count, STATES, HEADS, HEAD_DIM)
    )
    grad_summary_values = jnp.einsum(
        "lhst,lshd->lthd", summary_weights, grad_update, preferred_element_type=jnp.float32
    )
    grad_summary_weights = jnp.einsum(
        "lshd,lthd->lhst", grad_update, own_values, preferred_element_type=jnp.float32
    )
    summary_inner = jnp.sum(summary_probs * grad_summary_weights, axis=-1, keepdims=True)
    grad_summary_scores = (summary_probs * (grad_summary_weights - summary_inner)).astype(
        jnp.bfloat16
    )
    grad_state_query = (
        jnp.einsum(
            "lhst,lthd->shd", grad_summary_scores, own_keys, preferred_element_type=jnp.float32
        ).reshape(STATES, D)
        * score_scale
    )
    grad_summary_keys = (
        jnp.einsum(
            "lhst,shd->lthd", grad_summary_scores, query_state, preferred_element_type=jnp.float32
        )
        * score_scale
    )
    grad_summary = jnp.stack([grad_summary_keys, grad_summary_values], axis=2)
    grad_qkv_rows = jnp.concatenate([grad_queries[:, :, None], grad_own + grad_summary], axis=2)
    grad_qkv_rows = grad_qkv_rows.reshape(token_rows, 3 * D).astype(jnp.bfloat16)
    grad_qkv = jnp.dot(normed.T, grad_qkv_rows, preferred_element_type=jnp.float32)
    grad_normed = jnp.dot(grad_qkv_rows, qkv_weight.T, preferred_element_type=jnp.float32)
    grad_tok_norm, grad_norm_gain = norm_back(tokens, norm_gain, grad_normed)
    grad_tokens = grad_residual + grad_tok_norm
    grad_table = jnp.dot(
        onehot.astype(jnp.float32).T,
        grad_tokens,
        precision=highest,
        preferred_element_type=jnp.float32,
    )
    grad_distance_bias = bias_fold(jnp.sum(grad_bias_lanes.astype(jnp.float32), axis=0))
    shards = (
        lax.psum_scatter(grad_table, "seq", scatter_dimension=0, tiled=True),
        lax.psum_scatter(grad_norm_gain, "seq", scatter_dimension=0, tiled=True),
        lax.psum_scatter(grad_qkv, "seq", scatter_dimension=0, tiled=True),
        lax.psum_scatter(grad_distance_bias, "seq", scatter_dimension=0, tiled=True),
        lax.psum_scatter(grad_state_query, "seq", scatter_dimension=0, tiled=True),
        lax.psum_scatter(grad_state_init, "seq", scatter_dimension=0, tiled=True),
        lax.psum_scatter(grad_state_gain, "seq", scatter_dimension=0, tiled=True),
        lax.psum_scatter(grad_state_kv, "seq", scatter_dimension=0, tiled=True),
        lax.psum_scatter(grad_gate, "seq", scatter_dimension=0, tiled=True),
        lax.psum_scatter(grad_out, "seq", scatter_dimension=0, tiled=True),
        lax.psum_scatter(grad_mlp_gain, "seq", scatter_dimension=0, tiled=True),
        lax.psum_scatter(grad_up, "seq", scatter_dimension=0, tiled=True),
        lax.psum_scatter(grad_down, "seq", scatter_dimension=0, tiled=True),
    )
    summed = (
        lax.psum(shards[0].astype(jnp.bfloat16), "dp").astype(jnp.float32),
        lax.psum(shards[1].astype(jnp.bfloat16), "dp").astype(jnp.float32),
        lax.psum(shards[2].astype(jnp.bfloat16), "dp").astype(jnp.float32),
        lax.psum(shards[3].astype(jnp.bfloat16), "dp").astype(jnp.float32),
        lax.psum(shards[4].astype(jnp.bfloat16), "dp").astype(jnp.float32),
        lax.psum(shards[5].astype(jnp.bfloat16), "dp").astype(jnp.float32),
        lax.psum(shards[6].astype(jnp.bfloat16), "dp").astype(jnp.float32),
        lax.psum(shards[7].astype(jnp.bfloat16), "dp").astype(jnp.float32),
        lax.psum(shards[8].astype(jnp.bfloat16), "dp").astype(jnp.float32),
        lax.psum(shards[9].astype(jnp.bfloat16), "dp").astype(jnp.float32),
        lax.psum(shards[10].astype(jnp.bfloat16), "dp").astype(jnp.float32),
        lax.psum(shards[11].astype(jnp.bfloat16), "dp").astype(jnp.float32),
        lax.psum(shards[12].astype(jnp.bfloat16), "dp").astype(jnp.float32),
    )
    return (
        layer_out,
        summed[0],
        summed[1],
        summed[2],
        summed[3],
        summed[4],
        summed[5],
        summed[6],
        summed[7],
        summed[8],
        summed[9],
        summed[10],
        summed[11],
        summed[12],
    )


def solution(mesh):
    placed = (
        P("dp", "seq"),
        P("dp", "seq"),
        P(),
        P(),
        P(),
        P(),
        P(),
        P(),
        P(),
        P(),
        P(),
        P(),
        P(),
        P(),
        P(),
        P("dp", "seq", None),
    )
    return jax.shard_map(
        body,
        mesh=mesh,
        in_specs=placed,
        out_specs=(
            P("dp", "seq", None),
            P("seq", None),
            P("seq"),
            P("seq", None),
            P("seq"),
            P("seq", None),
            P("seq", None),
            P("seq"),
            P("seq", None),
            P("seq"),
            P("seq", None),
            P("seq"),
            P("seq", None),
            P("seq", None),
        ),
        check_vma=False,
    )
```

profile of v0, /device:TPU:0, one launch (start us, length us, event | category | flops | bytes accessed | tf_op | source)
XLA Modules:
  0.0 1402.7 jit_solution(12140151972453591108)
XLA Ops:
  63.8 17.0 %slice.68 = f32[8,785920]{1,0:T(8,128)} slice(f32[8,786432]{1,0:T(8,128)} %bitcast.240), slice={[0:8], [0:785920]} | slice | bytes 50298880 | tf_op jit(solution)/shard_map/slice | solution.py:111
  80.8 18.8 %reshape.392 = f32[6287360]{0:T(1024)} reshape(f32[8,785920]{1,0:T(8,128)} %slice.68) | data formatting | bytes 50298880
  99.5 39.4 %reshape.364 = f32[8,512,1535]{2,1,0:T(8,128)} reshape(f32[6287360]{0:T(1024)} %reshape.392) | data formatting | bytes 50298880 | tf_op jit(solution)/shard_map/reshape | solution.py:112
  152.3 20.6 %all-gather = f32[8192]{0:T(1024)S(1)} all-gather(f32[1024]{0:T(1024)S(1)} %get-tuple-element.420), channel_id=2, replica_groups=mesh['dp'=4,'seq'=8] {'seq'}, dimensions={0}, use_global_device_ids=true | all-gather | bytes 36864 | tf_op jit(solution)/shard_map/all_gather | solution.py:32
  174.3 35.4 %all-gather.7.cloned.1.call-done = f32[4096,1024]{1,0:T(8,128)} async-done(((f32[512,1024]{1,0:T(8,128)}), f32[4096,1024]{1,0:T(8,128)}) %all-gather.7.cloned.1.call-update) | async-done | bytes 16777232 | tf_op jit(solution)/shard_map/all_gather | solution.py:32
  209.6 33.2 %while.20 = (s32[]{:T(128)}, f32[1,512,1024]{2,1,0:T(8,128)}, s32[]{:T(128)}, f32[8,1,1024]{2,1,0:T(1,128)S(1)}, f32[8,1,512,1024]{3,2,1,0:T(8,128)}, /*index=5*/s32[]{:T(128)}, s32[]{:T(128)}) while((s32[]{:T(128)}, f32[1,512,1024]{2,1,0:T(8,128)}, s32[]{:T(128)}, f32[8,1,1024]{2,1,0:T(1,128)S(1)}, f32[8,1,512,1024]{3,2,1,0:T(8,128)}, ...), condition=%wide.region_5.6_spmd.clone, body=%wide.region_4.5_spmd.clone.sunk | while | flops 2097156 | bytes 6303857 | solution.py:44
  254.9 15.6 %fusion.89 = (f32[8,512]{1,0:T(8,128)S(1)}, f32[8,512,1536]{2,1,0:T(8,128)}) fusion(f32[8,512,1024]{2,1,0:T(8,128)} %slice.69, bf16[1536,2,8,128]{3,0,2,1:T(8,128)(2,1)} %maximum_bitcast_fusion.1, bf16[1,512,1,8,128]{4,3,2,1,0:T(8,128)(2,1)S(1)} %copy-done.16, pred[512,1536]{1,0:T(8,128)(4,1)} %add_add_fusion.3), kind=kOutput, calls=%fused_computation.163 | convolution fusion | flops 1635774464 | bytes 46940160 | tf_op jit(solution)/shard_map/while/body/eval_jaxpr/qhd,khd->hqk/dot_general | solution.py:134
  309.3 15.0 %fusion.14 = bf16[512,4096]{1,0:T(8,128)(2,1)} fusion(f32[512,4096]{1,0:T(8,128)} %fusion.79, bf16[4096,1024]{1,0:T(8,128)(2,1)} %param.40, bf16[1,512,1024]{2,1,0:T(8,128)(2,1)S(1)} %copy-done.20), kind=kOutput, calls=%fused_computation.27 | convolution fusion | flops 4336910336 | bytes 22020096 | tf_op jit(solution)/shard_map/dot_general | solution.py:240
  351.9 17.0 %multiply_reduce_fusion = (f32[8,512]{1,0:T(8,128)S(1)}, f32[8,512,1536]{2,1,0:T(8,128)}) fusion(f32[8,512,1536]{2,1,0:T(8,128)} %get-tuple-element.440, f32[8,512]{1,0:T(8,128)S(1)} %log_add_fusion, bf16[512,8,128]{0,2,1:T(8,128)(2,1)S(1)} %bitcast.249, bf16[1536,2,8,128]{3,0,2,1:T(8,128)(2,1)} %maximum_bitcast_fusion.1), kind=kOutput, calls=%fused_computation.8 | convolution fusion | flops 1629483008 | bytes 54558720 | tf_op jit(solution)/shard_map/while/body/eval_jaxpr/qhd,khd->hqk/dot_general | solution.py:264
  368.9 17.0 %multiply_convert_fusion = bf16[8,512,1536]{2,1,0:T(8,128)(2,1)S(1)} fusion(f32[8,512,1536]{2,1,0:T(8,128)} %get-tuple-element.445, f32[8,512,1536]{2,1,0:T(8,128)} %get-tuple-element.440, f32[8,512]{1,0:T(8,128)S(1)} %get-tuple-element.444, f32[8,512]{1,0:T(8,128)S(1)} %log_add_fusion), kind=kLoop, calls=%fused_computation.7 | loop fusion | flops 25165824 | bytes 62947328 | tf_op jit(solution)/shard_map/while/body/eval_jaxpr/convert_element_type | solution.py:268
  431.5 15.6 %all-gather.2 = bf16[8192]{0:T(1024)(128)(2,1)S(1)} all-gather(bf16[1024]{0:T(1024)(128)(2,1)S(1)} %copy-done.64), channel_id=4, replica_groups=mesh['dp'=4,'seq'=8] {'seq'}, dimensions={0}, use_global_device_ids=true | all-gather | bytes 18432 | tf_op jit(solution)/shard_map/all_gather | solution.py:50
  461.5 51.6 %all-gather.9.cloned.1.call-done = bf16[8,512,1024]{2,1,0:T(8,128)(2,1)} async-done(((bf16[1,512,1024]{2,1,0:T(8,128)(2,1)}), bf16[8,512,1024]{2,1,0:T(8,128)(2,1)}) %all-gather.9.cloned.1.call-update) | async-done | bytes 8388624 | tf_op jit(solution)/shard_map/all_gather | solution.py:50
  513.1 20.6 %while.42 = (s32[]{:T(128)}, f32[1,512,1024]{2,1,0:T(8,128)S(1)}, s32[]{:T(128)}, bf16[8,1,1024]{2,1,0:T(2,128)(2,1)S(1)}, bf16[8,1,512,1024]{3,2,1,0:T(8,128)(2...) while((s32[]{:T(128)}, f32[1,512,1024]{2,1,0:T(8,128)S(1)}, s32[]{:T(128)}, ...), condition=%wide.region_18.19_spmd.clone, body=%wide.region_17.18_spmd.clone.sunk | while | flops 2622472 | bytes 5253295 | solution.py:68
  579.1 15.0 %fusion.52 = f32[4096,1024]{1,0:T(8,128)} fusion(bf16[1,512,1024]{2,1,0:T(8,128)(2,1)S(1)} %copy-done.22, f32[512,4096]{1,0:T(8,128)} %fusion.79), kind=kOutput, calls=%fused_computation.108 | convolution fusion | flops 4313841664 | bytes 26214400 | tf_op jit(solution)/shard_map/dot_general | solution.py:239
  619.0 48.5 %reduce-scatter.17.cloned.1.call-done = f32[128,2048]{1,0:T(8,128)} async-done(((f32[1024,2048]{1,0:T(8,128)}), f32[128,2048]{1,0:T(8,128)}) %reduce-scatter.17.cloned.1.call-update) | async-done | bytes 1048592 | tf_op jit(solution)/shard_map/reduce_scatter | solution.py:351
  669.5 31.5 %reduce-scatter.9.cloned.1.call-done = f32[32,1024]{1,0:T(8,128)} async-done(((f32[256,1024]{1,0:T(8,128)}), f32[32,1024]{1,0:T(8,128)}) %reduce-scatter.9.cloned.1.call-update) | async-done | bytes 131088 | tf_op jit(solution)/shard_map/reduce_scatter | solution.py:344
  702.5 34.5 %reduce-scatter.15.cloned.1.call-done = f32[64,1024]{1,0:T(8,128)} async-done(((f32[512,1024]{1,0:T(8,128)}), f32[64,1024]{1,0:T(8,128)}) %reduce-scatter.15.cloned.1.call-update) | async-done | bytes 262160 | tf_op jit(solution)/shard_map/reduce_scatter | solution.py:349
  738.7 35.2 %reduce-scatter.13.cloned.1.call-done = f32[64,1024]{1,0:T(8,128)} async-done(((f32[512,1024]{1,0:T(8,128)}), f32[64,1024]{1,0:T(8,128)}) %reduce-scatter.13.cloned.1.call-update) | async-done | bytes 262160 | tf_op jit(solution)/shard_map/reduce_scatter | solution.py:348
  775.5 167.6 %reduce-scatter.23.cloned.1.call-done = f32[512,1024]{1,0:T(8,128)} async-done(((f32[4096,1024]{1,0:T(8,128)}), f32[512,1024]{1,0:T(8,128)}) %reduce-scatter.23.cloned.1.call-update) | async-done | bytes 2097168 | tf_op jit(solution)/shard_map/reduce_scatter | solution.py:356
  945.8 166.3 %reduce-scatter.21.cloned.1.call-done = f32[128,4096]{1,0:T(8,128)} async-done(((f32[1024,4096]{1,0:T(8,128)}), f32[128,4096]{1,0:T(8,128)}) %reduce-scatter.21.cloned.1.call-update) | async-done | bytes 2097168 | tf_op jit(solution)/shard_map/reduce_scatter | solution.py:355
  1114.8 127.1 %reduce-scatter.11.cloned.1.call-done = f32[128,3072]{1,0:T(8,128)} async-done(((f32[1024,3072]{1,0:T(8,128)}), f32[128,3072]{1,0:T(8,128)}) %reduce-scatter.11.cloned.1.call-update) | async-done | bytes 1572880 | tf_op jit(solution)/shard_map/reduce_scatter | solution.py:346
  1267.5 22.5 %reshape.394 = bf16[6287360]{0:T(1024)(128)(2,1)} reshape(bf16[8,512,1535]{2,1,0:T(8,128)(2,1)} %concatenate.33) | data formatting | bytes 25149440
  1290.0 22.9 %reshape.370 = bf16[8,785920]{1,0:T(8,128)(2,1)} reshape(bf16[6287360]{0:T(1024)(128)(2,1)} %reshape.394) | data formatting | bytes 25149440 | tf_op jit(solution)/shard_map/reshape | solution.py:117
  1343.7 26.0 %all-reduce.8 = (bf16[1024]{0:T(1024)(128)(2,1)S(1)}, bf16[256]{0:T(256)(128)(2,1)S(1)}, bf16[1024]{0:T(1024)(128)(2,1)S(1)}, bf16[1024]{0:T(1024)(128)(2,1)S(1)}, bf16[1024]{0:T(1024)(128)(2,1)S(1)}) all-reduce(f32[1024]{0:T(1024)S(1)} %get-tuple-element.375, f32[256]{0:T(256)S(1)} %reshape.373, ...), channel_id=7, replica_groups=mesh['dp'=4,'seq'=8] {'seq'}, use_global_device_ids=true, to_apply=%region_25.26.clone | all-reduce | flops 4352 | bytes 26112
  (351 shorter events, 425.2 us)
Async XLA Ops:
  7.2 287.7 %copy-start = (bf16[1024,1024]{1,0:T(8,128)(2,1)S(1)}, bf16[1024,1024]{1,0:T(8,128)(2,1)}, u32[]{:S(2)}) copy-start(bf16[1024,1024]{1,0:T(8,128)(2,1)} %param.37) | copy-start | bytes 6291460
  7.2 202.4 %all-gather.7.cloned.1.call-start = ((), (), s32[]{:S(2)}) async-start(), calls=%async_computation.16 | async-start | bytes 18874368 | tf_op jit(solution)/shard_map/all_gather | solution.py:32
  9.5 15.9 %copy-start.13 = (bf16[512,1024]{0,1:T(8,128)(2,1)}, bf16[512,1024]{0,1:T(8,128)(2,1)S(1)}, u32[]{:S(2)}) copy-start(bf16[512,1024]{0,1:T(8,128)(2,1)S(1)} %copy.126) | copy-start | bytes 3145732
  42.1 471.0 %all-gather.9.cloned.1.call-start = ((), (), s32[]{:S(2)}) async-start(), calls=%async_computation.17 | async-start | bytes 9437184 | tf_op jit(solution)/shard_map/all_gather | solution.py:50
  46.0 203.5 %collective-permute-start = (bf16[1,512,2,8,128]{4,1,3,2,0:T(8,128)(2,1)}, bf16[1,512,2,8,128]{4,1,3,2,0:T(8,128)(2,1)}, u32[]{:S(2)}, u32[]{:S(2)}) collective-permute-start(bf16[1,512,2,8,128]{4,1,3,2,0:T(8,128)(2,1)} %copy.122), channel_id=1, source_target_pairs={{0,1},{1,2},{2,3},{3,4},{4,5},{5,6},{6,7},{8,9},{9,10},{10,11},{11... | collective-permute-start | bytes 6291464 | tf_op jit(solution)/shard_map/ppermute | solution.py:27
  139.0 34.0 %copy-start.34 = (pred[512,512]{1,0:T(32,128)(4,1)S(1)}, pred[512,512]{1,0:T(32,128)(4,1)}, u32[]{:S(2)}) copy-start(pred[512,512]{1,0:T(32,128)(4,1)} %constant.190.clone) | copy-start | bytes 786436
  139.0 34.1 %copy-start.33 = (pred[512,512]{1,0:T(32,128)(4,1)S(1)}, pred[512,512]{1,0:T(32,128)(4,1)}, u32[]{:S(2)}) copy-start(pred[512,512]{1,0:T(32,128)(4,1)} %constant.191.clone) | copy-start | bytes 786436
  298.1 33.8 %copy-start.17 = (f32[512,1024]{1,0:T(8,128)}, f32[512,1024]{1,0:T(8,128)S(1)}, u32[]{:S(2)}) copy-start(f32[512,1024]{1,0:T(8,128)S(1)} %get-tuple-element.442) | copy-start | bytes 6291460
  298.2 33.8 %copy-start.47 = (f32[512]{0:T(512)}, f32[512]{0:T(512)S(1)}, u32[]{:S(2)}) copy-start(f32[512]{0:T(512)S(1)} %broadcast_multiply_fusion.1) | copy-start | bytes 6148
  298.5 33.5 %copy-start.60 = (f32[512]{0:T(512)}, f32[512]{0:T(512)S(1)}, u32[]{:S(2)}) copy-start(f32[512]{0:T(512)S(1)} %fusion.71) | copy-start | bytes 6148
  298.5 25.7 %slice-start.2 = ((s8[8388608]{0:T(1024)(128)(4,1)}), s8[4194304]{0:T(1024)(128)(4,1)S(1)}, s32[]{:S(2)}) async-start(s8[8388608]{0:T(1024)(128)(4,1)} %bitcast.267), calls=%async_computation.21 | async-start | bytes 8388608
  418.3 198.8 %reduce-scatter.19.cloned.1.call-start = ((), (), s32[]{:S(2)}) async-start(), calls=%async_computation.13 | async-start | bytes 4718592 | tf_op jit(solution)/shard_map/reduce_scatter | solution.py:353
  423.0 244.5 %reduce-scatter.17.cloned.1.call-start = ((), (), s32[]{:S(2)}) async-start(), calls=%async_computation.12 | async-start | bytes 9437184 | tf_op jit(solution)/shard_map/reduce_scatter | solution.py:351
  430.9 270.1 %reduce-scatter.9.cloned.1.call-start = ((), (), s32[]{:S(2)}) async-start(), calls=%async_computation.8 | async-start | bytes 1179648 | tf_op jit(solution)/shard_map/reduce_scatter | solution.py:344
  450.1 104.4 %collective-permute-start.1 = (bf16[1,512,2,8,128]{1,4,3,2,0:T(8,128)(2,1)}, bf16[1,512,2,8,128]{1,4,3,2,0:T(8,128)(2,1)}, u32[]{:S(2)}, u32[]{:S(2)}) collective-permute-start(bf16[1,512,2,8,128]{1,4,3,2,0:T(8,128)(2,1)} %get-tuple-element.425), channel_id=1, source_target_pairs={{1,0},{2,1},{3,2},{4,3},{5,4},{6,5},{7,6},{9,8},{10,9},{11,10},{12... | collective-permute-start | bytes 6291464 | tf_op jit(solution)/shard_map/ppermute | solution.py:27
  513.1 20.6 %copy-start.42 = (f32[1024]{0:T(1024)S(1)}, f32[1024]{0:T(1024)}, u32[]{:S(2)}) copy-start(f32[1024]{0:T(1024)} %copy-done.41) | copy-start | bytes 12292
  513.1 20.6 %copy-start.44 = (f32[1024]{0:T(1024)S(1)}, f32[1024]{0:T(1024)}, u32[]{:S(2)}) copy-start(f32[1024]{0:T(1024)} %copy-done.43) | copy-start | bytes 12292
  570.0 167.1 %reduce-scatter.15.cloned.1.call-start = ((), (), s32[]{:S(2)}) async-start(), calls=%async_computation.11 | async-start | bytes 2359296 | tf_op jit(solution)/shard_map/reduce_scatter | solution.py:349
  570.6 203.3 %reduce-scatter.13.cloned.1.call-start = ((), (), s32[]{:S(2)}) async-start(), calls=%async_computation.10 | async-start | bytes 2359296 | tf_op jit(solution)/shard_map/reduce_scatter | solution.py:348
  578.7 364.4 %reduce-scatter.23.cloned.1.call-start = ((), (), s32[]{:S(2)}) async-start(), calls=%async_computation.15 | async-start | bytes 18874368 | tf_op jit(solution)/shard_map/reduce_scatter | solution.py:356
  594.2 518.0 %reduce-scatter.21.cloned.1.call-start = ((), (), s32[]{:S(2)}) async-start(), calls=%async_computation.14 | async-start | bytes 18874368 | tf_op jit(solution)/shard_map/reduce_scatter | solution.py:355
  608.2 633.7 %reduce-scatter.11.cloned.1.call-start = ((), (), s32[]{:S(2)}) async-start(), calls=%async_computation.9 | async-start | bytes 14155776 | tf_op jit(solution)/shard_map/reduce_scatter | solution.py:346
  616.9 765.6 %all-reduce.13.cloned.1.call-start = ((), (), s32[]{:S(2)}) async-start(), calls=%async_computation.18 | async-start | bytes 7995392 | tf_op jit(solution)/shard_map/psum | solution.py:359
  1114.8 129.5 %copy-start.76 = (u32[32]{0:T(128)S(1)}, u32[32]{0:T(128)}, u32[]{:S(2)}) copy-start(u32[32]{0:T(128)} %constant.203) | copy-start | bytes 388
  (72 other events, 327.6 us)
Sparse Core Ops, SparseCore 0:
  42.2 167.3 all-gather.6
  418.5 94.5 all-gather.8
  515.4 62.0 reduce-scatter.18
  579.6 87.7 reduce-scatter.16
  670.1 30.8 reduce-scatter.8
  703.1 33.8 reduce-scatter.14
  739.4 34.5 reduce-scatter.12
  776.3 166.8 reduce-scatter.22
  945.5 166.5 reduce-scatter.20
  1114.3 127.5 reduce-scatter.10
  1247.5 101.5 all-reduce.12
where the time goes:
time: 1410 us; the launch traced here: 1400 us
  waiting for transfers between devices  698 us (50%)
  local copies, waits for them, and re-layouts  232 us (16%)
  matrix products  215 us (15%)
  other arithmetic  162 us (11%)
  blocking collectives  72 us (5%)
  between operations  17.4 us (1%)
    reduce_scatter x1, waiting for transfers between devices, body(): lax.psum_scatter(grad_down, 'seq', scatter_dimension=0, tiled=True)  168 us
    reduce_scatter x1, waiting for transfers between devices, body(): lax.psum_scatter(grad_up, 'seq', scatter_dimension=0, tiled=True)  166 us
    reduce_scatter x1, waiting for transfers between devices, body(): lax.psum_scatter(grad_qkv, 'seq', scatter_dimension=0, tiled=True)  127 us
    unnamed x178, local copies, waits for them, and re-layouts  69.3 us
    select_n x16, other arithmetic, lap(): return jax.tree.map(lambda a, b: jnp.where(reached, a, b), new, before)  53.4 us
    all_gather x1, waiting for transfers between devices, entering_2(): lax.all_gather(part.astype(kind), axis)  51.6 us
    reduce_scatter x1, waiting for transfers between devices, body(): lax.psum_scatter(grad_state_kv, 'seq', scatter_dimension=0, tiled=True)  48.5 us
    reshape x1, local copies, waits for them, and re-layouts, bias_matrix(): return tiled.reshape(HEADS, WINDOW, 3 * WINDOW - 1)[:, :, WINDOW - 1:]  39.4 us
  transfers between devices with their start and end apart: 13, of which 9 were waited for; matrix products, arithmetic and copies ran while one was open for 27% of the time, Pallas kernels for 0%

commit v1 on v0

v1 whole, which is shorter than its diff:
```python
import functools
import math

import jax
import jax.numpy as jnp
import numpy as np
from jax import lax
from jax.experimental import pallas as pl
from jax.experimental.pallas import tpu as pltpu
from jax.sharding import PartitionSpec as P

D = 1024
HEADS = 8
HEAD_DIM = 128
FF = 4096
VOCAB = 256
STATES = 512
WINDOW = 512
BUCKETS = 32
MAX_DISTANCE = 128
CONTEXT = 2 * WINDOW
TILE = 256
SPLITS = 2

epsilon = 1e-05
hidden = -1e30
log2e = math.log2(math.e)
score_scale = 1.0 / math.sqrt(HEAD_DIM)
f32 = jnp.float32
bf16 = jnp.bfloat16

NN = (((1,), (0,)), ((), ()))
NT = (((1,), (1,)), ((), ()))
TN = (((0,), (0,)), ((), ()))


def dot(a, b, dims=NN):
    return lax.dot_general(a, b, dims, preferred_element_type=f32)


def params(mib=48):
    return pltpu.CompilerParams(
        dimension_semantics=("arbitrary",), vmem_limit_bytes=mib * 1024 * 1024
    )


def cost(flops, moved, exps=0):
    return pl.CostEstimate(
        flops=int(flops), bytes_accessed=int(moved), transcendentals=int(exps)
    )


def norm_parts(value):
    centre = jnp.mean(value, axis=-1, keepdims=True)
    offset = value - centre
    spread = jnp.mean(offset * offset, axis=-1, keepdims=True)
    inv = lax.rsqrt(spread + epsilon)
    return offset * inv, inv


def norm_back(unit, inv, gain, upstream):
    scaled = upstream * gain
    a = jnp.mean(scaled, axis=-1, keepdims=True)
    b = jnp.mean(scaled * unit, axis=-1, keepdims=True)
    return (scaled - a - unit * b) * inv


def bucket_table():
    distance = np.arange(WINDOW)
    exact_count = BUCKETS // 2
    log_ratio = np.log(np.maximum(distance, 1) / exact_count) / math.log(
        MAX_DISTANCE / exact_count
    )
    far_bucket = exact_count + np.floor(log_ratio * (BUCKETS - exact_count)).astype(
        np.int64
    )
    return np.where(
        distance < exact_count, distance, np.minimum(far_bucket, BUCKETS - 1)
    )


def lane_pick():
    pick = np.zeros((BUCKETS, CONTEXT), np.float32)
    table = bucket_table()
    for m in range(1, WINDOW + 1):
        pick[table[WINDOW - m], m] = 1.0
    return pick


def lane_hidden():
    m = np.arange(CONTEXT)
    return np.where((m >= 1) & (m <= WINDOW), 0.0, hidden).astype(np.float32)[None]


def summary_forward_kernel(
    span, sq, kt, vt, lnn, init, fcol, state_out, y_out, lse_out, lg, a_s, y_s
):
    kt_h = kt[...]
    vtr = vt[...].astype(f32).T.astype(bf16)
    lg[...] = dot(kt_h, sq[...], NT) * (score_scale * log2e)
    a_s[...] = init[...].astype(f32).T
    y_s[...] = jnp.zeros_like(y_s)
    f = jnp.concatenate([fcol[...]] * (STATES // 128), axis=1)

    def step(w, _):
        n = lnn[w]
        x = lg[...] + jnp.concatenate([n] * (STATES // 128), axis=1)
        m = jnp.max(x, axis=0, keepdims=True)
        p = jnp.exp2(x - m)
        z = jnp.sum(p, axis=0, keepdims=True)
        u = dot(vtr, p.astype(bf16)) * (1.0 / z)
        lse_out[0, pl.ds(w, 1), :] = m + jnp.log2(z)
        a = a_s[...]
        y_s[...] = a - u + f * y_s[...]
        a_s[...] = u + f * (a - u)
        return 0

    lax.fori_loop(span[0], span[1], step, 0)
    state_out[...] = a_s[...].T
    y_out[...] = y_s[...].T


def summary_forward(span, state_query, qkv_table, lnn, state_init, fcol):
    windows = lnn.shape[0]
    head = lambda k: (lambda h, s: (0, k * HEADS + h))
    return pl.pallas_call(
        summary_forward_kernel,
        grid_spec=pltpu.PrefetchScalarGridSpec(
            num_scalar_prefetch=1,
            grid=(HEADS,),
            in_specs=[
                pl.BlockSpec((STATES, HEAD_DIM), head(0)),
                pl.BlockSpec((VOCAB, HEAD_DIM), head(1)),
                pl.BlockSpec((VOCAB, HEAD_DIM), head(2)),
                pl.BlockSpec((windows, VOCAB, 128), lambda h, s: (0, 0, 0)),
                pl.BlockSpec((STATES, HEAD_DIM), head(0)),
                pl.BlockSpec((HEAD_DIM, 128), lambda h, s: (h, 0)),
            ],
            out_specs=[
                pl.BlockSpec((STATES, HEAD_DIM), head(0)),
                pl.BlockSpec((STATES, HEAD_DIM), head(0)),
                pl.BlockSpec((1, windows, STATES), lambda h, s: (h, 0, 0)),
            ],
            scratch_shapes=[
                pltpu.VMEM((VOCAB, STATES), f32),
                pltpu.VMEM((HEAD_DIM, STATES), f32),
                pltpu.VMEM((HEAD_DIM, STATES), f32),
            ],
        ),
        out_shape=[
            jax.ShapeDtypeStruct((STATES, D), f32),
            jax.ShapeDtypeStruct((STATES, D), f32),
            jax.ShapeDtypeStruct((HEADS, windows, STATES), f32),
        ],
        compiler_params=params(),
        cost_estimate=cost(4e9, 8e6, 8e6),
        name="summary_forward",
    )(span, state_query, qkv_table, qkv_table, lnn, state_init, fcol)


def summary_backward_kernel(
    span,
    sq,
    kt,
    vt,
    lnn,
    lse,
    local,
    fcol,
    gk_in,
    gv_in,
    gk_out,
    gv_out,
    gsq_out,
    ginit_out,
    lg,
    g_s,
    gs_s,
    gv_s,
):
    kt_h = kt[...]
    vt_h = vt[...]
    sq_h = sq[...]
    lg[...] = dot(kt_h, sq_h, NT) * (score_scale * log2e)
    g_s[...] = local[...].T
    gs_s[...] = jnp.zeros_like(gs_s)
    gv_s[...] = gv_in[...]
    f = jnp.concatenate([fcol[...]] * (STATES // 128), axis=1)
    first, here = span[0], span[1]

    def step(t, _):
        w = here - 1 - t
        g = g_s[...]
        fg = f * g
        gu = (g - fg).astype(bf16)
        g_s[...] = fg
        n = lnn[w]
        p = jnp.exp2(
            lg[...]
            + jnp.concatenate([n] * (STATES // 128), axis=1)
            - lse[0, pl.ds(w, 1), :]
        )
        dw = dot(vt_h, gu)
        pd = p * dw
        inner = jnp.sum(pd, axis=0, keepdims=True)
        gs_s[...] += pd - p * inner
        gv_s[...] += dot(p.astype(bf16), gu, NT)
        return 0

    lax.fori_loop(0, here - first, step, 0)
    gs = (gs_s[...] * score_scale).astype(bf16)
    gk_out[...] = (gk_in[...] + dot(gs, sq_h)).astype(bf16)
    gv_out[...] = gv_s[...].astype(bf16)
    gsq_out[...] = dot(gs, kt_h, TN).astype(bf16)
    ginit_out[...] = g_s[...].T.astype(bf16)


def summary_backward(span, state_query, qkv_table, lnn, lse, local, fcol, gk, gv):
    windows = lnn.shape[0]
    head = lambda k: (lambda h, s: (0, k * HEADS + h))
    table = pl.BlockSpec((VOCAB, HEAD_DIM), head(0))
    states = pl.BlockSpec((STATES, HEAD_DIM), head(0))
    return pl.pallas_call(
        summary_backward_kernel,
        grid_spec=pltpu.PrefetchScalarGridSpec(
            num_scalar_prefetch=1,
            grid=(HEADS,),
            in_specs=[
                states,
                pl.BlockSpec((VOCAB, HEAD_DIM), head(1)),
                pl.BlockSpec((VOCAB, HEAD_DIM), head(2)),
                pl.BlockSpec((windows, VOCAB, 128), lambda h, s: (0, 0, 0)),
                pl.BlockSpec((1, windows, STATES), lambda h, s: (h, 0, 0)),
                states,
                pl.BlockSpec((HEAD_DIM, 128), lambda h, s: (h, 0)),
                table,
                table,
            ],
            out_specs=[table, table, states, states],
            scratch_shapes=[
                pltpu.VMEM((VOCAB, STATES), f32),
                pltpu.VMEM((HEAD_DIM, STATES), f32),
                pltpu.VMEM((VOCAB, STATES), f32),
                pltpu.VMEM((VOCAB, HEAD_DIM), f32),
            ],
        ),
        out_shape=[
            jax.ShapeDtypeStruct((VOCAB, D), bf16),
            jax.ShapeDtypeStruct((VOCAB, D), bf16),
            jax.ShapeDtypeStruct((STATES, D), bf16),
            jax.ShapeDtypeStruct((STATES, D), bf16),
        ],
        compiler_params=params(),
        cost_estimate=cost(8e9, 8e6, 8e6),
        name="summary_backward",
    )(span, state_query, qkv_table, qkv_table, lnn, lse, local, fcol, gk, gv)


def bias_tile(row):
    spread = jnp.broadcast_to(row, (TILE, CONTEXT))
    shifted = pltpu.roll(spread, 0, 1, stride=1, stride_axis=0)
    return shifted[:, : 3 * TILE].T


def attention_forward_kernel(
    live, pick, pick_t, qt, kt, vt, sk, sv, bias_row, mixed_out, lse_out, bias
):
    bias[...] = bias_tile(bias_row[0])
    prev_add = jnp.where(live[0] > 0, 0.0, hidden).astype(f32)
    keys = dot(pick[...], kt[...]).astype(bf16)
    values_t = dot(vt[...], pick_t[...], TN).astype(bf16)
    query = dot(pick[WINDOW:, :], qt[...]).astype(bf16)
    state_values_t = sv[...].astype(f32).T.astype(bf16)
    for j in range(WINDOW // TILE):
        q = query[j * TILE : (j + 1) * TILE]
        scores = []
        for rel in range(3):
            kt_i = j + rel
            s = (
                dot(keys[kt_i * TILE : (kt_i + 1) * TILE], q, NT)
                * (score_scale * log2e)
                + bias[rel * TILE : (rel + 1) * TILE]
            )
            if kt_i * TILE < WINDOW:
                s = s + prev_add
            scores.append(s)
        for st in range(STATES // TILE):
            scores.append(
                dot(sk[st * TILE : (st + 1) * TILE, :], q, NT) * (score_scale * log2e)
            )
        peak = functools.reduce(
            jnp.maximum, [jnp.max(s, axis=0, keepdims=True) for s in scores]
        )
        total = jnp.zeros((1, TILE), f32)
        out = jnp.zeros((HEAD_DIM, TILE), f32)
        for i, s in enumerate(scores):
            p = jnp.exp2(s - peak)
            total = total + jnp.sum(p, axis=0, keepdims=True)
            if i < 3:
                v = values_t[:, (j + i) * TILE : (j + i + 1) * TILE]
            else:
                v = state_values_t[:, (i - 3) * TILE : (i - 2) * TILE]
            out = out + dot(v, p.astype(bf16))
        out = out * (1.0 / total)
        mixed_out[j * TILE : (j + 1) * TILE, :] = out.T.astype(bf16)
        lse_out[0, :, j * TILE : (j + 1) * TILE] = peak + jnp.log2(total)


def attention_forward(live, pick, pick_t, qkv_table, sk, sv, bias_rows):
    head = lambda k: (lambda h, s: (0, k * HEADS + h))
    whole = lambda *shape: pl.BlockSpec(shape, lambda h, s: (0,) * len(shape))
    return pl.pallas_call(
        attention_forward_kernel,
        grid_spec=pltpu.PrefetchScalarGridSpec(
            num_scalar_prefetch=1,
            grid=(HEADS,),
            in_specs=[
                whole(CONTEXT, VOCAB),
                whole(VOCAB, CONTEXT),
                pl.BlockSpec((VOCAB, HEAD_DIM), head(0)),
                pl.BlockSpec((VOCAB, HEAD_DIM), head(1)),
                pl.BlockSpec((VOCAB, HEAD_DIM), head(2)),
                pl.BlockSpec((STATES, HEAD_DIM), head(0)),
                pl.BlockSpec((STATES, HEAD_DIM), head(1)),
                pl.BlockSpec((1, 1, CONTEXT), lambda h, s: (h, 0, 0)),
            ],
            out_specs=[
                pl.BlockSpec((WINDOW, HEAD_DIM), head(0)),
                pl.BlockSpec((1, 1, WINDOW), lambda h, s: (h, 0, 0)),
            ],
            scratch_shapes=[pltpu.VMEM((3 * TILE, TILE), f32)],
        ),
        out_shape=[
            jax.ShapeDtypeStruct((WINDOW, D), bf16),
            jax.ShapeDtypeStruct((HEADS, 1, WINDOW), f32),
        ],
        compiler_params=params(),
        cost_estimate=cost(6e9, 8e6, 6e6),
        name="attention_forward",
    )(live, pick, pick_t, qkv_table, qkv_table, qkv_table, sk, sv, bias_rows)


def attention_backward_kernel(
    live,
    pick,
    pick_t,
    qt,
    kt,
    vt,
    sk,
    sv,
    bias_row,
    lse,
    mixed,
    grad,
    gq_out,
    gk_out,
    gv_out,
    gsk_out,
    gsv_out,
    fold_out,
    bias,
    bias_grad,
):
    bias[...] = bias_tile(bias_row[0])
    bias_grad[...] = jnp.zeros_like(bias_grad)
    prev_add = jnp.where(live[0] > 0, 0.0, hidden).astype(f32)
    keys = dot(pick[...], kt[...]).astype(bf16)
    keys_t = dot(kt[...], pick_t[...], TN).astype(bf16)
    values = dot(pick[...], vt[...]).astype(bf16)
    query = dot(pick[WINDOW:, :], qt[...]).astype(bf16)
    state_keys_t = sk[...].astype(f32).T.astype(bf16)
    inner_all = jnp.sum(
        (mixed[...].astype(f32) * grad[...].astype(f32)).T, axis=0, keepdims=True
    )
    blocks = WINDOW // TILE
    gq = [jnp.zeros((HEAD_DIM, TILE), f32) for _ in range(blocks)]
    gk = jnp.zeros((VOCAB, HEAD_DIM), f32)
    gv = jnp.zeros((VOCAB, HEAD_DIM), f32)

    def piece(k, k_t, v, j, add, bias_at):
        rows = slice(j * TILE, (j + 1) * TILE)
        q = query[rows]
        g = grad[rows, :]
        s = dot(k, q, NT) * (score_scale * log2e)
        if bias_at is not None:
            s = s + bias[bias_at * TILE : (bias_at + 1) * TILE]
        shift = lse[0, :, rows]
        if add:
            shift = shift - prev_add
        p = jnp.exp2(s - shift)
        dp = dot(v, g, NT)
        gs = p * (dp - inner_all[:, rows])
        gs16 = gs.astype(bf16)
        gq[j] = gq[j] + dot(k_t, gs16)
        if bias_at is not None:
            bias_grad[bias_at * TILE : (bias_at + 1) * TILE] += gs
        return dot(gs16, q), dot(p.astype(bf16), g)

    for st in range(STATES // TILE):
        at = slice(st * TILE, (st + 1) * TILE)
        parts = [
            piece(sk[at, :], state_keys_t[:, at], sv[at, :], j, False, None)
            for j in range(blocks)
        ]
        gsk_out[at, :] = (sum(p[0] for p in parts) * score_scale).astype(bf16)
        gsv_out[at, :] = sum(p[1] for p in parts).astype(bf16)
    for tile in range(CONTEXT // TILE):
        at = slice(tile * TILE, (tile + 1) * TILE)
        parts = [
            piece(keys[at], keys_t[:, at], values[at], j, tile * TILE < WINDOW, tile - j)
            for j in range(blocks)
            if 0 <= tile - j < 3
        ]
        one = pick_t[:, at]
        gk = gk + dot(one, (sum(p[0] for p in parts) * score_scale).astype(bf16))
        gv = gv + dot(one, sum(p[1] for p in parts).astype(bf16))
    gk_out[...] = gk
    gv_out[...] = gv
    total = jnp.zeros((HEAD_DIM, VOCAB), f32)
    for j in range(blocks):
        rows = slice(WINDOW + j * TILE, WINDOW + (j + 1) * TILE)
        total = total + dot((gq[j] * score_scale).astype(bf16), pick[rows, :])
    gq_out[...] = total.T.astype(bf16)
    rows = jnp.concatenate(
        [bias_grad[...].T, jnp.zeros((TILE, CONTEXT - 3 * TILE), f32)], axis=1
    )
    count = TILE
    while count > 8:
        count //= 2
        rows = rows[:count] + pltpu.roll(rows[count:], CONTEXT - count, 1)
    folded = rows[0:1]
    for r in range(1, 8):
        folded = folded + pltpu.roll(rows, CONTEXT - r, 1)[r : r + 1]
    fold_out[0] = folded


def attention_backward(
    live, pick, pick_t, qkv_table, sk, sv, bias_rows, lse, mixed, grad
):
    head = lambda k: (lambda h, s: (0, k * HEADS + h))
    whole = lambda *shape: pl.BlockSpec(shape, lambda h, s: (0,) * len(shape))
    table = pl.BlockSpec((VOCAB, HEAD_DIM), head(0))
    tokens = pl.BlockSpec((WINDOW, HEAD_DIM), head(0))
    states = pl.BlockSpec((STATES, HEAD_DIM), head(0))
    return pl.pallas_call(
        attention_backward_kernel,
        grid_spec=pltpu.PrefetchScalarGridSpec(
            num_scalar_prefetch=1,
            grid=(HEADS,),
            in_specs=[
                whole(CONTEXT, VOCAB),
                whole(VOCAB, CONTEXT),
                pl.BlockSpec((VOCAB, HEAD_DIM), head(0)),
                pl.BlockSpec((VOCAB, HEAD_DIM), head(1)),
                pl.BlockSpec((VOCAB, HEAD_DIM), head(2)),
                pl.BlockSpec((STATES, HEAD_DIM), head(0)),
                pl.BlockSpec((STATES, HEAD_DIM), head(1)),
                pl.BlockSpec((1, 1, CONTEXT), lambda h, s: (h, 0, 0)),
                pl.BlockSpec((1, 1, WINDOW), lambda h, s: (h, 0, 0)),
                tokens,
                tokens,
            ],
            out_specs=[
                table,
                table,
                table,
                states,
                states,
                pl.BlockSpec((1, 1, CONTEXT), lambda h, s: (h, 0, 0)),
            ],
            scratch_shapes=[
                pltpu.VMEM((3 * TILE, TILE), f32),
                pltpu.VMEM((3 * TILE, TILE), f32),
            ],
        ),
        out_shape=[
            jax.ShapeDtypeStruct((VOCAB, D), bf16),
            jax.ShapeDtypeStruct((VOCAB, D), f32),
            jax.ShapeDtypeStruct((VOCAB, D), f32),
            jax.ShapeDtypeStruct((STATES, D), bf16),
            jax.ShapeDtypeStruct((STATES, D), bf16),
            jax.ShapeDtypeStruct((HEADS, 1, CONTEXT), f32),
        ],
        compiler_params=params(),
        cost_estimate=cost(14e9, 12e6, 6e6),
        name="attention_backward",
    )(
        live,
        pick,
        pick_t,
        qkv_table,
        qkv_table,
        qkv_table,
        sk,
        sv,
        bias_rows,
        lse,
        mixed,
        grad,
    )


def mlp_kernel(x, cot, up, down, out_in, gx_in, gd_out, gu_out, out, gx, xt):
    @pl.when(pl.program_id(0) == 0)
    def _():
        out[...] = out_in[...]
        gx[...] = gx_in[...]
        xt[...] = x[...].astype(f32).T.astype(bf16)

    up_b = up[...]
    down_b = down[...]
    pre = dot(x[...], up_b)
    root = math.sqrt(2.0 / math.pi)
    square = pre * pre
    t = jnp.tanh(root * pre * (1.0 + 0.044715 * square))
    half = 0.5 * (1.0 + t)
    act = (pre * half).astype(bf16)
    slope = half + (0.5 * root) * pre * (1.0 - t * t) * (1.0 + (3 * 0.044715) * square)
    grad_pre = (dot(cot[...], down_b, NT) * slope).astype(bf16)
    out[...] += dot(act, down_b)
    gx[...] += dot(grad_pre, up_b, NT)
    gd_out[...] = dot(act, cot[...], TN).astype(bf16)
    gu_out[...] = dot(xt[...], grad_pre).astype(bf16)


def mlp_part(part, x, cot, up, down, out, gx):
    count = FF // SPLITS // TILE
    whole = pl.BlockSpec((WINDOW, D), lambda s: (0, 0))
    return pl.pallas_call(
        mlp_kernel,
        grid=(count,),
        in_specs=[
            whole,
            whole,
            pl.BlockSpec((D, TILE), lambda s: (0, SPLITS * s + part)),
            pl.BlockSpec((TILE, D), lambda s: (SPLITS * s + part, 0)),
            whole,
            whole,
        ],
        out_specs=[
            pl.BlockSpec((TILE, D), lambda s: (s, 0)),
            pl.BlockSpec((D, TILE), lambda s: (0, s)),
            whole,
            whole,
        ],
        out_shape=[
            jax.ShapeDtypeStruct((count * TILE, D), bf16),
            jax.ShapeDtypeStruct((D, count * TILE), bf16),
            jax.ShapeDtypeStruct((WINDOW, D), f32),
            jax.ShapeDtypeStruct((WINDOW, D), f32),
        ],
        scratch_shapes=[pltpu.VMEM((D, WINDOW), bf16)],
        compiler_params=params(),
        cost_estimate=cost(6 * 2 * WINDOW * D * FF // SPLITS, 40e6 / SPLITS, 1e6),
        name="feed_forward",
    )(x, cot, up, down, out, gx)


def permute(value, axis, to):
    size = lax.axis_size(axis)
    return lax.ppermute(value, axis, [(i, to(i)) for i in range(size)])


def halves(value, which, dim):
    size = value.shape[dim] // 2
    keep = lax.dynamic_slice_in_dim(value, which * size, size, dim)
    send = lax.dynamic_slice_in_dim(value, (1 - which) * size, size, dim)
    return keep, send


def joined(mine, other, which, dim):
    first = jnp.where(which == 0, mine, other)
    second = jnp.where(which == 0, other, mine)
    return jnp.concatenate([first, second], axis=dim)


def fitted():
    return lax.axis_size("seq") == 8 and lax.axis_size("dp") == 4


def total_of(value, order):
    rows = value.shape[1]
    if not fitted():
        flat = value.reshape((-1,) + value.shape[2:])
        own = lax.psum_scatter(flat, "seq", scatter_dimension=0, tiled=True)
        return lax.psum(own, "dp").astype(f32)
    here = lax.axis_index("seq")
    core, depth = here % 2, here // 2
    dp = lax.axis_index("dp")
    places = (dp % 2, dp // 2)
    pairs = value.reshape((4, 2) + value.shape[1:])
    keep = lax.dynamic_index_in_dim(pairs, core, 1, False)
    send = lax.dynamic_index_in_dim(pairs, 1 - core, 1, False)
    value = keep + permute(send, "seq", lambda i: i ^ 1)
    for axis in order:
        keep, send = halves(value, places[axis], 1)
        value = keep + permute(send, "dp", lambda i, axis=axis: i ^ (1 << axis))
    own = lax.dynamic_index_in_dim(value, depth, 0, False).astype(f32)
    for step in (1, 2, 3):
        send = lax.dynamic_index_in_dim(value, (depth + step) % 4, 0, False)
        came = permute(send, "seq", lambda i, step=step: (i + 2 * step) % 8)
        own = own + came.astype(f32)
    own = own.astype(bf16)
    for axis in reversed(order):
        other = permute(own, "dp", lambda i, axis=axis: i ^ (1 << axis))
        own = joined(own, other, places[axis], 0)
    return own.astype(f32)


def gathered(own):
    if not fitted():
        return lax.all_gather(own, "seq", tiled=True)
    here = lax.axis_index("seq")
    core, depth = here % 2, here // 2
    both = joined(own[None], permute(own, "seq", lambda i: i ^ 1)[None], core, 0)
    parts = [both] + [
        permute(both, "seq", lambda i, step=step: (i - 2 * step) % 8)
        for step in (1, 2, 3)
    ]
    ring = jnp.concatenate(parts, axis=0)
    ring = jnp.concatenate([ring, ring], axis=0)
    return lax.dynamic_slice_in_dim(ring, (8 - 2 * depth) % 8, 8, 0).reshape(
        (-1,) + own.shape[1:]
    )


def body(
    char_ids,
    seg_starts,
    char_table,
    norm_gain,
    qkv_weight,
    distance_bias,
    state_query,
    state_init,
    state_gain,
    state_kv_weight,
    gate_logit,
    out_weight,
    mlp_gain,
    up_weight,
    down_weight,
    cotangent,
):
    windows = lax.axis_size("seq")
    here = lax.axis_index("seq")
    shard = lambda n: n // windows

    packed = jnp.concatenate(
        [char_ids.reshape(4, 128), jnp.broadcast_to(seg_starts, (1, 128))], axis=0
    )
    everyone = lax.all_gather(packed, "seq")
    ids_all = everyone[:, :4].reshape(windows, WINDOW)
    flags = everyone[:, 4, 0]
    order = jnp.arange(windows, dtype=jnp.int32)
    first = jnp.max(jnp.where((flags > 0) & (order <= here), order, 0))
    span = jnp.stack([first, here]).astype(jnp.int32)
    live = (1 - seg_starts.reshape(1)).astype(jnp.int32)
    vocab = jnp.arange(VOCAB, dtype=jnp.int32)
    counts = jnp.sum(
        (ids_all[:, :, None] == vocab[None, None, :]).astype(f32), axis=1
    )
    lnn = jnp.where(counts > 0, jnp.log2(jnp.maximum(counts, 1.0)), hidden)
    lnn = jnp.broadcast_to(lnn[:, :, None], (windows, VOCAB, 128))
    before = lax.dynamic_index_in_dim(ids_all, jnp.maximum(here - 1, 0), 0, False)
    context_ids = jnp.concatenate([before, char_ids.reshape(-1)])
    pick = (context_ids[:, None] == vocab[None, :]).astype(bf16)
    pick_t = (vocab[:, None] == context_ids[None, :]).astype(bf16)

    table = char_table.astype(f32)
    table_unit, table_inv = norm_parts(table)
    normed_table = (table_unit * norm_gain).astype(bf16)
    qkv_table = dot(normed_table, qkv_weight).astype(bf16)

    forget = jax.nn.sigmoid(gate_logit)
    fcol = jnp.broadcast_to(forget[:, None], (D, 128))
    states_in, forget_slope, summary_lse = summary_forward(
        span, state_query, qkv_table, lnn, state_init, fcol
    )
    state_unit, state_inv = norm_parts(states_in)
    state_normed = (state_unit * state_gain).astype(bf16)
    state_kv = dot(state_normed, state_kv_weight).astype(bf16)

    bias_rows = (
        jnp.dot(
            distance_bias.reshape(HEADS, BUCKETS),
            jnp.asarray(lane_pick()),
            precision=lax.Precision.HIGHEST,
        )
        * log2e
        + jnp.asarray(lane_hidden())
    ).reshape(HEADS, 1, CONTEXT)
    mixed, lse = attention_forward(
        live, pick, pick_t, qkv_table, state_kv, state_kv, bias_rows
    )
    own_pick = pick[WINDOW:]
    residual = dot(own_pick, char_table) + dot(mixed, out_weight)
    mlp_unit, mlp_inv = norm_parts(residual)
    mlp_in = (mlp_unit * mlp_gain).astype(bf16)
    upstream = cotangent.reshape(WINDOW, D)

    out, gx = residual, jnp.zeros((WINDOW, D), f32)
    grads_down, grads_up = [], []
    for part in range(SPLITS):
        gd, gu, out, gx = mlp_part(part, mlp_in, upstream, up_weight, down_weight, out, gx)
        grads_down.append(gd)
        grads_up.append(gu)
    layer_out = out.astype(bf16).reshape(1, WINDOW, D)

    grad_mlp_gain = jnp.sum(gx * mlp_unit, axis=0)
    grad_residual = upstream.astype(f32) + norm_back(mlp_unit, mlp_inv, mlp_gain, gx)
    grad_attention = grad_residual.astype(bf16)
    grad_out = dot(mixed, grad_attention, TN).astype(bf16)
    grad_mixed = dot(grad_attention, out_weight, NT).astype(bf16)
    rows_sum = dot(own_pick, grad_attention, TN).astype(bf16)

    gq, gk, gv, gsk, gsv, fold = attention_backward(
        live, pick, pick_t, qkv_table, state_kv, state_kv, bias_rows, lse, mixed, grad_mixed
    )
    grad_state_kv = [
        dot(state_normed, gsk, TN).astype(bf16),
        dot(state_normed, gsv, TN).astype(bf16),
    ]
    grad_state_normed = dot(gsk, state_kv_weight[:, :D], NT) + dot(
        gsv, state_kv_weight[:, D:], NT
    )
    grad_state_gain = jnp.sum(grad_state_normed * state_unit, axis=0)
    local = norm_back(state_unit, state_inv, state_gain, grad_state_normed)
    grad_gate = jnp.sum(local * forget_slope, axis=0) * forget * (1.0 - forget)
    grad_distance = lax.dot_general(
        fold.reshape(HEADS, CONTEXT),
        jnp.asarray(lane_pick()),
        NT,
        precision=lax.Precision.HIGHEST,
        preferred_element_type=f32,
    ).reshape(-1)
    gk, gv, gsq, ginit = summary_backward(
        span, state_query, qkv_table, lnn, summary_lse, local, fcol, gk, gv
    )

    own_down, own_up = [], []
    for part in range(SPLITS):
        order = (0, 1) if part % 2 == 0 else (1, 0)
        if fitted():
            gd = grads_down[part].reshape(windows, -1, D)
            gu = grads_up[part].reshape(windows, shard(D), -1)
            own_down.append(total_of(gd, order))
            own_up.append(total_of(gu, order))
    if fitted():
        grad_down = jnp.concatenate(own_down, axis=0)
        grad_up = jnp.stack(
            [part.reshape(shard(D), -1, TILE) for part in own_up], axis=2
        ).reshape(shard(D), FF)
    else:
        full = jnp.stack([g.reshape(-1, TILE, D) for g in grads_down], axis=1)
        grad_down = total_of(full.reshape(windows, -1, D), (0, 1))
        full = jnp.stack([g.reshape(D, -1, TILE) for g in grads_up], axis=2)
        grad_up = total_of(full.reshape(windows, shard(D), FF), (0, 1))
    middle = jnp.concatenate(
        [
            grad_out.reshape(windows, shard(D), D),
            rows_sum.reshape(windows, shard(VOCAB), D),
        ],
        axis=1,
    )
    middle = total_of(middle, (0, 1))
    grad_out = middle[: shard(D)]
    rows_sum = middle[shard(D) :]
    grad_state_kv = jnp.concatenate(
        [g.reshape(windows, shard(D), D) for g in grad_state_kv], axis=1
    )
    grad_state_kv = total_of(grad_state_kv, (1, 0))
    grad_state_kv = jnp.concatenate(
        [grad_state_kv[: shard(D)], grad_state_kv[shard(D) :]], axis=1
    )
    small = jnp.concatenate(
        [
            g.reshape(windows, -1)
            for g in (grad_mlp_gain, grad_state_gain, grad_gate, grad_distance)
        ],
        axis=1,
    ).astype(bf16)
    used = small.shape[1]
    small = jnp.pad(small, ((0, 0), (0, 32 * D - used))).reshape(windows, 32, D)
    last = jnp.concatenate(
        [
            gsq.reshape(windows, shard(STATES), D),
            ginit.reshape(windows, shard(STATES), D),
            gq.reshape(windows, shard(VOCAB), D),
            gk.reshape(windows, shard(VOCAB), D),
            gv.reshape(windows, shard(VOCAB), D),
            small,
        ],
        axis=1,
    )
    last = total_of(last, (0, 1))
    cuts = np.cumsum([shard(STATES), shard(STATES)] + [shard(VOCAB)] * 3)
    grad_state_query, grad_state_init, gq, gk, gv, small = jnp.split(last, cuts, axis=0)
    small = small.reshape(-1)
    span_d = shard(D)
    grad_mlp_gain = small[:span_d]
    grad_state_gain = small[span_d : 2 * span_d]
    grad_gate = small[2 * span_d : 3 * span_d]
    grad_distance = small[3 * span_d : 3 * span_d + shard(HEADS * BUCKETS)]

    grad_rows = jnp.concatenate([gq, gk, gv], axis=1).astype(bf16)
    all_rows = gathered(grad_rows)
    mine = lax.dynamic_slice_in_dim(normed_table, here * span_d, span_d, 1)
    grad_qkv = dot(mine, all_rows, TN)
    weight_rows = lax.dynamic_slice_in_dim(qkv_weight, here * span_d, span_d, 0)
    unit_cols = lax.dynamic_slice_in_dim(table_unit, here * span_d, span_d, 1)
    grad_norm_gain = jnp.sum(dot(all_rows, weight_rows, NT) * unit_cols, axis=0)
    grad_normed = dot(grad_rows, qkv_weight, NT)
    at = here * shard(VOCAB)
    grad_table = rows_sum + norm_back(
        lax.dynamic_slice_in_dim(table_unit, at, shard(VOCAB), 0),
        lax.dynamic_slice_in_dim(table_inv, at, shard(VOCAB), 0),
        norm_gain,
        grad_normed,
    )
    return (
        layer_out,
        grad_table,
        grad_norm_gain,
        grad_qkv,
        grad_distance,
        grad_state_query,
        grad_state_init,
        grad_state_gain,
        grad_state_kv,
        grad_gate,
        grad_out,
        grad_mlp_gain,
        grad_up,
        grad_down,
    )


def solution(mesh):
    placed = (P("dp", "seq"), P("dp", "seq")) + (P(),) * 13 + (P("dp", "seq", None),)
    return jax.shard_map(
        body,
        mesh=mesh,
        in_specs=placed,
        out_specs=(
            P("dp", "seq", None),
            P("seq", None),
            P("seq"),
            P("seq", None),
            P("seq"),
            P("seq", None),
            P("seq", None),
            P("seq"),
            P("seq", None),
            P("seq"),
            P("seq", None),
            P("seq"),
            P("seq", None),
            P("seq", None),
        ),
        check_vma=False,
    )
```

time: 1410 us -> 546 us (0.39)
  waiting for transfers between devices: 698 us -> 169 us
  local copies, waits for them, and re-layouts: 232 us -> 44 us
  matrix products: 215 us -> 33.4 us
  Pallas kernels: 0 us -> 113 us
  other arithmetic: 162 us -> 54 us
  starting transfers between devices: 6.36 us -> 104 us
  blocking collectives: 72 us -> 15.7 us
    reduce_scatter x8 -> x0, waiting for transfers between devices: 611 us -> none  [the longest x1 168 us: body(): lax.psum_scatter(grad_down, 'seq', scatter_dimension=0, tiled=True)]
    dot_general x31 -> x16, matrix products: 215 us -> 33.4 us  [the longest x14 33 us: dot(): return lax.dot_general(a, b, dims, preferred_element_type=f32)]
    ppermute x2 -> x60, waiting for transfers between devices: 0.01 us -> 169 us  [permute(): return lax.ppermute(value, axis, [(i, to(i)) for i in range(size)])]
    pallas_call x0 -> x6, Pallas kernels: none -> 113 us  [the longest x2 43 us: mlp_part(): pl.pallas_call(mlp_kernel, grid=(count,), in_specs=[whole, whole, pl.Bloc...]
    ppermute x2 -> x60, starting transfers between devices: 5.33 us -> 104 us  [permute(): return lax.ppermute(value, axis, [(i, to(i)) for i in range(size)])]
    all_gather x2 -> x0, waiting for transfers between devices: 87 us -> none  [the longest x1 51.6 us: entering_2(): lax.all_gather(part.astype(kind), axis)]
    reshape x8 -> x3, local copies, waits for them, and re-layouts: 70.4 us -> 1.99 us  [the longest x1 1.89 us: body(): grad_up = jnp.stack([part.reshape(shard(D), -1, TILE) for part in own_up]...]
    select_n x16 -> x15, other arithmetic: 53.4 us -> 0.89 us  [the longest x14 0.88 us: joined(): first = jnp.where(which == 0, mine, other)]
  transfers between devices with their start and end apart: 13 -> 60, of which waited for: 9 -> 25; matrix products, arithmetic and copies ran while one was open for 27% -> 14% of each run, Pallas kernels for 0% -> 13%
where the time goes in v1:
time: 546 us; the launch traced here: 537 us
  waiting for transfers between devices  169 us (31%)
  Pallas kernels  113 us (21%)
  starting transfers between devices  104 us (19%)
  other arithmetic  54 us (10%)
  local copies, waits for them, and re-layouts  44 us (8%)
  matrix products  33.4 us (6%)
  blocking collectives  15.7 us (3%)
    ppermute x60, waiting for transfers between devices, permute(): return lax.ppermute(value, axis, [(i, to(i)) for i in range(size)])  169 us
    ppermute x60, starting transfers between devices, permute(): return lax.ppermute(value, axis, [(i, to(i)) for i in range(size)])  104 us
    pallas_call x2, Pallas kernels, mlp_part(): pl.pallas_call(mlp_kernel, grid=(count,), in_specs=[whole, whole, pl.Bloc...  43 us
    pallas_call x1, Pallas kernels, attention_backward(): pl.pallas_call(attention_backward_kernel, grid_spec=pltpu.PrefetchScalarG...  38.1 us
    dot_general x14, matrix products, dot(): return lax.dot_general(a, b, dims, preferred_element_type=f32)  33 us
    unnamed x144, local copies, waits for them, and re-layouts  23.1 us
    pallas_call x1, Pallas kernels, attention_forward(): pl.pallas_call(attention_forward_kernel, grid_spec=pltpu.PrefetchScalarGr...  17.1 us
    all_gather x1, blocking collectives, body(): everyone = lax.all_gather(packed, 'seq')  15.7 us
  transfers between devices with their start and end apart: 60, of which 25 were waited for; matrix products, arithmetic and copies ran while one was open for 14% of the time, Pallas kernels for 13%

profile of v1, /device:TPU:0, one launch (start us, length us, event | category | flops | bytes accessed | tf_op | source)
XLA Modules:
  0.0 537.3 jit_solution(15261437726077040819)
XLA Ops:
  2.3 15.7 %all-gather.1 = s32[8,5,128]{2,1,0:T(8,128)S(1)} all-gather(s32[1,5,128]{2,1,0:T(8,128)S(1)} %pad_bitcast_fusion), channel_id=2, replica_groups=mesh['dp'=4,'seq'=8] {'seq'}, dimensions={0}, use_global_device_ids=true | all-gather | bytes 23040 | tf_op jit(solution)/shard_map/all_gather | solution.py:653
  26.2 4.8 convolution_convert_fusion.kt.vt.qt
  31.6 6.2 %summary_forward.1 = (f32[512,1024]{1,0:T(8,128)}, f32[512,1024]{1,0:T(8,128)}, f32[8,8,512]{2,1,0:T(8,128)S(1)}) custom-call(s32[2]{0:T(128)S(1)} %pad_add_fusion.1.span, bf16[512,1024]{1,0:T(8,128)(2,1)S(1)} %copy-done.12, bf16[256,3072]{1,0:T(8,128)(2,1)S(1)} %convolution_convert_fusion.kt.vt.qt, bf16[256,3072]{1,0:T(8,128)(2,1)S(1)} %convolution_convert_fusion.kt.vt.qt, ...), custom_call_target="tpu_custom_call" | custom-call | flops 4000000000 | bytes 8000000 | tf_op jit(solution)/shard_map/summary_forward/pallas_call | solution.py:126
  42.2 4.9 convolution_convert_fusion.1.sk.sv
  47.2 17.1 %attention_forward.1 = (bf16[512,1024]{1,0:T(8,128)(2,1)S(1)}, f32[8,1,512]{2,1,0:T(1,128)S(1)}) custom-call(s32[1]{0:T(128)} %bitcast.5.live, bf16[1024,256]{1,0:T(8,128)(2,1)S(1)} %copy-done.5, bf16[256,1024]{1,0:T(8,128)(2,1)S(1)} %copy-done.9, bf16[256,3072]{1,0:T(8,128)(2,1)S(1)} %copy-done.21, bf16[256,3072]{1,0:T(8,128)(2,1)S(1)} %copy-done.21, ...), custom_call_target="tpu_custom_call" | custom-call | flops 6000000000 | bytes 8000000 | tf_op jit(solution)/shard_map/attention_forward/pallas_call | solution.py:312
  73.3 21.7 %feed_forward.2 = (bf16[2048,1024]{1,0:T(8,128)(2,1)}, bf16[1024,2048]{1,0:T(8,128)(2,1)}, f32[512,1024]{1,0:T(8,128)S(1)}, f32[512,1024]{1,0:T(8,128)}) custom-call(bf16[512,1024]{1,0:T(8,128)(2,1)S(1)} %multiply_convert_fusion.x, bf16[512,1024]{1,0:T(8,128)(2,1)S(1)} %bitcast.196, bf16[1024,4096]{1,0:T(8,128)(2,1)} %up.3, bf16[4096,1024]{1,0:T(8,128)(2,1)} %down.3, ...), custom_call_target="tpu_custom_call" | custom-call | flops 12884901888 | bytes 20000000 | tf_op jit(solution)/shard_map/feed_forward/pallas_call | solution.py:530
  95.0 3.9 dynamic-slice_bitcast_fusion.1
  102.9 21.3 %feed_forward.3 = (bf16[2048,1024]{1,0:T(8,128)(2,1)}, bf16[1024,2048]{1,0:T(8,128)(2,1)}, f32[512,1024]{1,0:T(8,128)S(1)}, f32[512,1024]{1,0:T(8,128)}) custom-call(bf16[512,1024]{1,0:T(8,128)(2,1)S(1)} %multiply_convert_fusion.x, bf16[512,1024]{1,0:T(8,128)(2,1)S(1)} %bitcast.197, bf16[1024,4096]{1,0:T(8,128)(2,1)} %up.3, bf16[4096,1024]{1,0:T(8,128)(2,1)} %down.3, ...), custom_call_target="tpu_custom_call" | custom-call | flops 12884901888 | bytes 20000000 | tf_op jit(solution)/shard_map/feed_forward/pallas_call | solution.py:530
  144.4 38.1 %attention_backward.1 = (bf16[256,1024]{1,0:T(8,128)(2,1)S(1)}, f32[256,1024]{1,0:T(8,128)S(1)}, f32[256,1024]{1,0:T(8,128)S(1)}, bf16[512,1024]{1,0:T(8,128)(2,...) custom-call(s32[1]{0:T(128)} %bitcast.5.live, bf16[1024,256]{1,0:T(8,128)(2,1)S(1)} %copy-done.6, ...), custom_call_target="tpu_custom_call" | custom-call | flops 14000000000 | bytes 12000000 | tf_op jit(solution)/shard_map/attention_backward/pallas_call | solution.py:446
  190.7 9.1 %summary_backward.1 = (bf16[256,1024]{1,0:T(8,128)(2,1)S(1)}, bf16[256,1024]{1,0:T(8,128)(2,1)S(1)}, bf16[512,1024]{1,0:T(8,128)(2,1)S(1)}, bf16[512,1024]{1,0:T(8,128)(2,1)S(1)}) custom-call(s32[2]{0:T(128)S(1)} %pad_add_fusion.1.span, bf16[512,1024]{1,0:T(8,128)(2,1)S(1)} %copy-done.13, bf16[256,3072]{1,0:T(8,128)(2,1)} %copy-done.20, ...), custom_call_target="tpu_custom_call" | custom-call | flops 8000000000 | bytes 8000000 | tf_op jit(solution)/shard_map/summary_backward/pallas_call | solution.py:223
  218.5 9.0 %collective-permute-done.1 = bf16[4,80,1024]{2,1,0:T(8,128)(2,1)} collective-permute-done((bf16[4,80,1024]{2,1,0:T(8,128)(2,1)}, bf16[4,80,1024]{2,1,0:T(8,128)(2,1)}, u32[]{:S(2)}, u32[]{:S(2)}) %collective-permute-start.1) | collective-permute-done | bytes 655392 | tf_op jit(solution)/shard_map/ppermute | solution.py:562
  243.7 11.8 %collective-permute-start.3 = (bf16[40,1024]{1,0:T(8,128)(2,1)S(1)}, bf16[40,1024]{1,0:T(8,128)(2,1)S(1)}, u32[]{:S(2)}, u32[]{:S(2)}) collective-permute-start(bf16[40,1024]{1,0:T(8,128)(2,1)S(1)} %get-tuple-element.154), channel_id=1, source_target_pairs={{0,2},{1,3},{2,4},{3,5},{4,6},{5,7},{6,0},{7,1},{8,10},{9,11},{10,... | collective-permute-start | bytes 245768 | tf_op jit(solution)/shard_map/ppermute | solution.py:562
  255.5 23.5 %collective-permute-start.5 = (bf16[40,1024]{1,0:T(8,128)(2,1)S(1)}, bf16[40,1024]{1,0:T(8,128)(2,1)S(1)}, u32[]{:S(2)}, u32[]{:S(2)}) collective-permute-start(bf16[40,1024]{1,0:T(8,128)(2,1)S(1)} %get-tuple-element.155), channel_id=1, source_target_pairs={{0,6},{1,7},{2,0},{3,1},{4,2},{5,3},{6,4},{7,5},{8,14},{9,15},{10,... | collective-permute-start | bytes 245768 | tf_op jit(solution)/shard_map/ppermute | solution.py:562
  291.1 40.2 %collective-permute-done.6 = bf16[40,1024]{1,0:T(8,128)(2,1)S(1)} collective-permute-done((bf16[40,1024]{1,0:T(8,128)(2,1)S(1)}, bf16[40,1024]{1,0:T(8,128)(2,1)S(1)}, u32[]{:S(2)}, u32[]{:S(2)}) %collective-permute-start.6) | collective-permute-done | bytes 81952 | tf_op jit(solution)/shard_map/ppermute | solution.py:562
  345.1 17.7 %collective-permute-done.21 = bf16[4,128,1024]{2,1,0:T(8,128)(2,1)S(1)} collective-permute-done((bf16[4,128,1024]{2,1,0:T(8,128)(2,1)S(1)}, bf16[4,128,1024]{2,1,0:T(8,128)(2,1)S(1)}, u32[]{:S(2)}, u32[]{:S(2)}) %collective-permute-start.21) | collective-permute-done | bytes 1048608 | tf_op jit(solution)/shard_map/ppermute | solution.py:562
  366.2 7.9 %collective-permute-done.46 = bf16[4,64,1024]{2,1,0:T(8,128)(2,1)S(1)} collective-permute-done((bf16[4,64,1024]{2,1,0:T(8,128)(2,1)S(1)}, bf16[4,64,1024]{2,1,0:T(8,128)(2,1)S(1)}, u32[]{:S(2)}, u32[]{:S(2)}) %collective-permute-start.46) | collective-permute-done | bytes 524320 | tf_op jit(solution)/shard_map/ppermute | solution.py:562
  375.6 9.7 %collective-permute-done.30 = bf16[4,32,2048]{2,1,0:T(8,128)(2,1)S(1)} collective-permute-done((bf16[4,32,2048]{2,1,0:T(8,128)(2,1)S(1)}, bf16[4,32,2048]{2,1,0:T(8,128)(2,1)S(1)}, u32[]{:S(2)}, u32[]{:S(2)}) %collective-permute-start.30) | collective-permute-done | bytes 524320 | tf_op jit(solution)/shard_map/ppermute | solution.py:562
  404.0 8.3 %collective-permute-done.32 = bf16[32,2048]{1,0:T(8,128)(2,1)S(1)} collective-permute-done((bf16[32,2048]{1,0:T(8,128)(2,1)S(1)}, bf16[32,2048]{1,0:T(8,128)(2,1)S(1)}, u32[]{:S(2)}, u32[]{:S(2)}) %collective-permute-start.32) | collective-permute-done | bytes 131104 | tf_op jit(solution)/shard_map/ppermute | solution.py:562
  415.4 4.4 collective-permute-start.55
  419.8 6.5 %collective-permute-done.40 = bf16[32,2048]{1,0:T(8,128)(2,1)S(1)} collective-permute-done((bf16[32,2048]{1,0:T(8,128)(2,1)S(1)}, bf16[32,2048]{1,0:T(8,128)(2,1)S(1)}, u32[]{:S(2)}, u32[]{:S(2)}) %collective-permute-start.40) | collective-permute-done | bytes 131104 | tf_op jit(solution)/shard_map/ppermute | solution.py:562
  433.7 4.5 collective-permute-start.11
  438.2 6.5 %collective-permute-done.56 = bf16[64,1024]{1,0:T(8,128)(2,1)S(1)} collective-permute-done((bf16[64,1024]{1,0:T(8,128)(2,1)S(1)}, bf16[64,1024]{1,0:T(8,128)(2,1)S(1)}, u32[]{:S(2)}, u32[]{:S(2)}) %collective-permute-start.56) | collective-permute-done | bytes 131104 | tf_op jit(solution)/shard_map/ppermute | solution.py:562
  465.9 12.8 %collective-permute-done.15 = bf16[128,1024]{1,0:T(8,128)(2,1)S(1)} collective-permute-done((bf16[128,1024]{1,0:T(8,128)(2,1)S(1)}, bf16[128,1024]{1,0:T(8,128)(2,1)S(1)}, u32[]{:S(2)}, u32[]{:S(2)}) %collective-permute-start.15) | collective-permute-done | bytes 262176 | tf_op jit(solution)/shard_map/ppermute | solution.py:562
  502.9 22.3 %collective-permute-done.18 = bf16[2,32,3072]{2,1,0:T(8,128)(2,1)S(1)} collective-permute-done((bf16[2,32,3072]{2,1,0:T(8,128)(2,1)}, bf16[2,32,3072]{2,1,0:T(8,128)(2,1)S(1)}, u32[]{:S(2)}, u32[]{:S(2)}) %collective-permute-start.18) | collective-permute-done | bytes 393248 | tf_op jit(solution)/shard_map/ppermute | solution.py:562
  (401 shorter events, 205.9 us)
Async XLA Ops:
  98.9 131.4 %collective-permute-start.44 = (bf16[4,256,1024]{2,1,0:T(8,128)(2,1)}, bf16[4,256,1024]{2,1,0:T(8,128)(2,1)}, u32[]{:S(2)}, u32[]{:S(2)}) collective-permute-start(bf16[4,256,1024]{2,1,0:T(8,128)(2,1)} %dynamic-slice_bitcast_fusion.1), channel_id=1, source_target_pairs={{0,1},{1,0},{2,3},{3,2},{4,5},{5,4},{6,7},{7,6},{8,9},{9,8},{10,11... | collective-permute-start | bytes 6291464 | tf_op jit(solution)/shard_map/ppermute | solution.py:562
  102.8 129.6 %collective-permute-start.28 = (bf16[4,128,2048]{2,1,0:T(8,128)(2,1)}, bf16[4,128,2048]{2,1,0:T(8,128)(2,1)}, u32[]{:S(2)}, u32[]{:S(2)}) collective-permute-start(bf16[4,128,2048]{2,1,0:T(8,128)(2,1)} %dynamic-slice_bitcast_fusion.3), channel_id=1, source_target_pairs={{0,1},{1,0},{2,3},{3,2},{4,5},{5,4},{6,7},{7,6},{8,9},{9,8},{10,11... | collective-permute-start | bytes 6291464 | tf_op jit(solution)/shard_map/ppermute | solution.py:562
  133.6 74.7 %collective-permute-start = (bf16[4,160,1024]{2,1,0:T(8,128)(2,1)}, bf16[4,160,1024]{2,1,0:T(8,128)(2,1)}, u32[]{:S(2)}, u32[]{:S(2)}) collective-permute-start(bf16[4,160,1024]{2,1,0:T(8,128)(2,1)} %fusion.13), channel_id=1, source_target_pairs={{0,1},{1,0},{2,3},{3,2},{4,5},{5,4},{6,7},{7,6},{8,9},{9,8},{10,11... | collective-permute-start | bytes 3932168 | tf_op jit(solution)/shard_map/ppermute | solution.py:562
  135.6 105.1 %collective-permute-start.52 = (bf16[4,256,1024]{2,1,0:T(8,128)(2,1)}, bf16[4,256,1024]{2,1,0:T(8,128)(2,1)}, u32[]{:S(2)}, u32[]{:S(2)}) collective-permute-start(bf16[4,256,1024]{2,1,0:T(8,128)(2,1)} %dynamic-slice_bitcast_fusion), channel_id=1, source_target_pairs={{0,1},{1,0},{2,3},{3,2},{4,5},{5,4},{6,7},{7,6},{8,9},{9,8},{10,11... | collective-permute-start | bytes 6291464 | tf_op jit(solution)/shard_map/ppermute | solution.py:562
  138.6 97.5 %collective-permute-start.36 = (bf16[4,128,2048]{2,1,0:T(8,128)(2,1)}, bf16[4,128,2048]{2,1,0:T(8,128)(2,1)}, u32[]{:S(2)}, u32[]{:S(2)}) collective-permute-start(bf16[4,128,2048]{2,1,0:T(8,128)(2,1)} %dynamic-slice_bitcast_fusion.2), channel_id=1, source_target_pairs={{0,1},{1,0},{2,3},{3,2},{4,5},{5,4},{6,7},{7,6},{8,9},{9,8},{10,11... | collective-permute-start | bytes 6291464 | tf_op jit(solution)/shard_map/ppermute | solution.py:562
  230.3 57.9 %collective-permute-start.8 = (bf16[4,256,1024]{2,1,0:T(8,128)(2,1)S(1)}, bf16[4,256,1024]{2,1,0:T(8,128)(2,1)S(1)}, u32[]{:S(2)}, u32[]{:S(2)}) collective-permute-start(bf16[4,256,1024]{2,1,0:T(8,128)(2,1)S(1)} %dynamic-slice_bitcast_fusion.4), channel_id=1, source_target_pairs={{0,1},{1,0},{2,3},{3,2},{4,5},{5,4},{6,7},{7,6},{8,9},{9,8},{10,11... | collective-permute-start | bytes 6291464 | tf_op jit(solution)/shard_map/ppermute | solution.py:562
  236.1 102.9 %collective-permute-start.45 = (bf16[4,128,1024]{2,1,0:T(8,128)(2,1)S(1)}, bf16[4,128,1024]{2,1,0:T(8,128)(2,1)S(1)}, u32[]{:S(2)}, u32[]{:S(2)}) collective-permute-start(bf16[4,128,1024]{2,1,0:T(8,128)(2,1)S(1)} %constant_dynamic-slice_fusion.3), channel_id=1, source_target_pairs={{0,8},{8,0},{16,24},{24,16},{1,9},{9,1},{17,25},{25,17},{2,10},{10... | collective-permute-start | bytes 3145736 | tf_op jit(solution)/shard_map/ppermute | solution.py:562
  243.7 38.4 %collective-permute-start.3 = (bf16[40,1024]{1,0:T(8,128)(2,1)S(1)}, bf16[40,1024]{1,0:T(8,128)(2,1)S(1)}, u32[]{:S(2)}, u32[]{:S(2)}) collective-permute-start(bf16[40,1024]{1,0:T(8,128)(2,1)S(1)} %get-tuple-element.154), channel_id=1, source_target_pairs={{0,2},{1,3},{2,4},{3,5},{4,6},{5,7},{6,0},{7,1},{8,10},{9,11},{10,... | collective-permute-start | bytes 245768 | tf_op jit(solution)/shard_map/ppermute | solution.py:562
  255.5 27.7 %collective-permute-start.5 = (bf16[40,1024]{1,0:T(8,128)(2,1)S(1)}, bf16[40,1024]{1,0:T(8,128)(2,1)S(1)}, u32[]{:S(2)}, u32[]{:S(2)}) collective-permute-start(bf16[40,1024]{1,0:T(8,128)(2,1)S(1)} %get-tuple-element.155), channel_id=1, source_target_pairs={{0,6},{1,7},{2,0},{3,1},{4,2},{5,3},{6,4},{7,5},{8,14},{9,15},{10,... | collective-permute-start | bytes 245768 | tf_op jit(solution)/shard_map/ppermute | solution.py:562
  282.1 58.0 %collective-permute-start.29 = (bf16[4,64,2048]{2,1,0:T(8,128)(2,1)S(1)}, bf16[4,64,2048]{2,1,0:T(8,128)(2,1)S(1)}, u32[]{:S(2)}, u32[]{:S(2)}) collective-permute-start(bf16[4,64,2048]{2,1,0:T(8,128)(2,1)S(1)} %constant_dynamic-slice_fusion.7), channel_id=1, source_target_pairs={{0,8},{8,0},{16,24},{24,16},{1,9},{9,1},{17,25},{25,17},{2,10},{10... | collective-permute-start | bytes 3145736 | tf_op jit(solution)/shard_map/ppermute | solution.py:562
  283.2 58.7 %collective-permute-start.53 = (bf16[4,128,1024]{2,1,0:T(8,128)(2,1)S(1)}, bf16[4,128,1024]{2,1,0:T(8,128)(2,1)S(1)}, u32[]{:S(2)}, u32[]{:S(2)}) collective-permute-start(bf16[4,128,1024]{2,1,0:T(8,128)(2,1)S(1)} %constant_dynamic-slice_fusion.1), channel_id=1, source_target_pairs={{0,16},{8,24},{16,0},{24,8},{1,17},{9,25},{17,1},{25,9},{2,18},{10... | collective-permute-start | bytes 3145736 | tf_op jit(solution)/shard_map/ppermute | solution.py:562
  287.1 56.1 %collective-permute-start.37 = (bf16[4,64,2048]{2,1,0:T(8,128)(2,1)S(1)}, bf16[4,64,2048]{2,1,0:T(8,128)(2,1)S(1)}, u32[]{:S(2)}, u32[]{:S(2)}) collective-permute-start(bf16[4,64,2048]{2,1,0:T(8,128)(2,1)S(1)} %constant_dynamic-slice_fusion.5), channel_id=1, source_target_pairs={{0,16},{8,24},{16,0},{24,8},{1,17},{9,25},{17,1},{25,9},{2,18},{10... | collective-permute-start | bytes 3145736 | tf_op jit(solution)/shard_map/ppermute | solution.py:562
  288.2 43.1 %collective-permute-start.6 = (bf16[40,1024]{1,0:T(8,128)(2,1)S(1)}, bf16[40,1024]{1,0:T(8,128)(2,1)S(1)}, u32[]{:S(2)}, u32[]{:S(2)}) collective-permute-start(bf16[40,1024]{1,0:T(8,128)(2,1)S(1)} %fusion.55), channel_id=1, source_target_pairs={{0,16},{8,24},{16,0},{24,8},{1,17},{9,25},{17,1},{25,9},{2,18},{10... | collective-permute-start | bytes 245768 | tf_op jit(solution)/shard_map/ppermute | solution.py:562
  336.7 26.1 %collective-permute-start.21 = (bf16[4,128,1024]{2,1,0:T(8,128)(2,1)S(1)}, bf16[4,128,1024]{2,1,0:T(8,128)(2,1)S(1)}, u32[]{:S(2)}, u32[]{:S(2)}) collective-permute-start(bf16[4,128,1024]{2,1,0:T(8,128)(2,1)S(1)} %constant_dynamic-slice_fusion.9), channel_id=1, source_target_pairs={{0,16},{8,24},{16,0},{24,8},{1,17},{9,25},{17,1},{25,9},{2,18},{10... | collective-permute-start | bytes 3145736 | tf_op jit(solution)/shard_map/ppermute | solution.py:562
  338.9 26.1 %collective-permute-start.9 = (bf16[4,128,1024]{2,1,0:T(8,128)(2,1)S(1)}, bf16[4,128,1024]{2,1,0:T(8,128)(2,1)S(1)}, u32[]{:S(2)}, u32[]{:S(2)}) collective-permute-start(bf16[4,128,1024]{2,1,0:T(8,128)(2,1)S(1)} %constant_dynamic-slice_fusion.12), channel_id=1, source_target_pairs={{0,8},{8,0},{16,24},{24,16},{1,9},{9,1},{17,25},{25,17},{2,10},{10... | collective-permute-start | bytes 3145736 | tf_op jit(solution)/shard_map/ppermute | solution.py:562
  340.1 34.0 %collective-permute-start.46 = (bf16[4,64,1024]{2,1,0:T(8,128)(2,1)S(1)}, bf16[4,64,1024]{2,1,0:T(8,128)(2,1)S(1)}, u32[]{:S(2)}, u32[]{:S(2)}) collective-permute-start(bf16[4,64,1024]{2,1,0:T(8,128)(2,1)S(1)} %constant_dynamic-slice_fusion.2), channel_id=1, source_target_pairs={{0,16},{8,24},{16,0},{24,8},{1,17},{9,25},{17,1},{25,9},{2,18},{10... | collective-permute-start | bytes 1572872 | tf_op jit(solution)/shard_map/ppermute | solution.py:562
  341.9 43.4 %collective-permute-start.30 = (bf16[4,32,2048]{2,1,0:T(8,128)(2,1)S(1)}, bf16[4,32,2048]{2,1,0:T(8,128)(2,1)S(1)}, u32[]{:S(2)}, u32[]{:S(2)}) collective-permute-start(bf16[4,32,2048]{2,1,0:T(8,128)(2,1)S(1)} %constant_dynamic-slice_fusion.6), channel_id=1, source_target_pairs={{0,16},{8,24},{16,0},{24,8},{1,17},{9,25},{17,1},{25,9},{2,18},{10... | collective-permute-start | bytes 1572872 | tf_op jit(solution)/shard_map/ppermute | solution.py:562
  343.2 46.7 %collective-permute-start.54 = (bf16[4,64,1024]{2,1,0:T(8,128)(2,1)S(1)}, bf16[4,64,1024]{2,1,0:T(8,128)(2,1)S(1)}, u32[]{:S(2)}, u32[]{:S(2)}) collective-permute-start(bf16[4,64,1024]{2,1,0:T(8,128)(2,1)S(1)} %constant_dynamic-slice_fusion), channel_id=1, source_target_pairs={{0,8},{8,0},{16,24},{24,16},{1,9},{9,1},{17,25},{25,17},{2,10},{10... | collective-permute-start | bytes 1572872 | tf_op jit(solution)/shard_map/ppermute | solution.py:562
  365.0 29.5 %collective-permute-start.22 = (bf16[4,64,1024]{2,1,0:T(8,128)(2,1)S(1)}, bf16[4,64,1024]{2,1,0:T(8,128)(2,1)S(1)}, u32[]{:S(2)}, u32[]{:S(2)}) collective-permute-start(bf16[4,64,1024]{2,1,0:T(8,128)(2,1)S(1)} %constant_dynamic-slice_fusion.8), channel_id=1, source_target_pairs={{0,8},{8,0},{16,24},{24,16},{1,9},{9,1},{17,25},{25,17},{2,10},{10... | collective-permute-start | bytes 1572872 | tf_op jit(solution)/shard_map/ppermute | solution.py:562
  385.3 41.1 %collective-permute-start.47 = (bf16[64,1024]{1,0:T(8,128)(2,1)S(1)}, bf16[64,1024]{1,0:T(8,128)(2,1)S(1)}, u32[]{:S(2)}, u32[]{:S(2)}) collective-permute-start(bf16[64,1024]{1,0:T(8,128)(2,1)S(1)} %get-tuple-element.122), channel_id=1, source_target_pairs={{0,2},{1,3},{2,4},{3,5},{4,6},{5,7},{6,0},{7,1},{8,10},{9,11},{10,... | collective-permute-start | bytes 393224 | tf_op jit(solution)/shard_map/ppermute | solution.py:562
  388.6 37.9 %collective-permute-start.49 = (bf16[64,1024]{1,0:T(8,128)(2,1)S(1)}, bf16[64,1024]{1,0:T(8,128)(2,1)S(1)}, u32[]{:S(2)}, u32[]{:S(2)}) collective-permute-start(bf16[64,1024]{1,0:T(8,128)(2,1)S(1)} %get-tuple-element.123), channel_id=1, source_target_pairs={{0,6},{1,7},{2,0},{3,1},{4,2},{5,3},{6,4},{7,5},{8,14},{9,15},{10,... | collective-permute-start | bytes 393224 | tf_op jit(solution)/shard_map/ppermute | solution.py:562
  457.8 27.5 %collective-permute-start.51 = (bf16[128,1024]{1,0:T(8,128)(2,1)S(1)}, bf16[128,1024]{1,0:T(8,128)(2,1)S(1)}, u32[]{:S(2)}, u32[]{:S(2)}) collective-permute-start(bf16[128,1024]{1,0:T(8,128)(2,1)S(1)} %pad_maximum_fusion.7), channel_id=1, source_target_pairs={{0,8},{8,0},{16,24},{24,16},{1,9},{9,1},{17,25},{25,17},{2,10},{10... | collective-permute-start | bytes 786440 | tf_op jit(solution)/shard_map/ppermute | solution.py:562
  493.4 31.8 %collective-permute-start.18 = (bf16[2,32,3072]{2,1,0:T(8,128)(2,1)}, bf16[2,32,3072]{2,1,0:T(8,128)(2,1)S(1)}, u32[]{:S(2)}, u32[]{:S(2)}) collective-permute-start(bf16[2,32,3072]{2,1,0:T(8,128)(2,1)} %pad_maximum_fusion.1), channel_id=1, source_target_pairs={{0,4},{1,5},{2,6},{3,7},{4,0},{5,1},{6,2},{7,3},{8,12},{9,13},{10,... | collective-permute-start | bytes 1179656 | tf_op jit(solution)/shard_map/ppermute | solution.py:562
  499.5 26.5 %collective-permute-start.19 = (bf16[2,32,3072]{2,1,0:T(8,128)(2,1)}, bf16[2,32,3072]{2,1,0:T(8,128)(2,1)S(1)}, u32[]{:S(2)}, u32[]{:S(2)}) collective-permute-start(bf16[2,32,3072]{2,1,0:T(8,128)(2,1)} %pad_maximum_fusion.1), channel_id=1, source_target_pairs={{0,2},{1,3},{2,4},{3,5},{4,6},{5,7},{6,0},{7,1},{8,10},{9,11},{10,... | collective-permute-start | bytes 1179656 | tf_op jit(solution)/shard_map/ppermute | solution.py:562
  (97 other events, 1005.2 us)
